TPU v7x, 32 devices: a whole 2x2x4 slice. The times are simulated.
32 devices in a mesh: wide: 8 (over y, x, core), narrow: 4 (over z).
Axes of the slice: x: 2, y: 2, z: 4, core: 2. Of those that a mesh axis runs over, the one named last changes fastest.
Arguments:
- tokens: bfloat16 [32768, 768], P(('wide', 'narrow')), may hold values from -6 to 6
- first_values: bfloat16 [32768, 384], P(('wide', 'narrow')), may hold values from -6 to 6
- cotangent: bfloat16 [32768, 768], P(('wide', 'narrow')), may hold values from -6 to 6
- attend_gain: bfloat16 [768], P(('wide', 'narrow')), may hold values from 0.5 to 1.5
- attend_shift: bfloat16 [768], P(('wide', 'narrow')), may hold values from -4 to 4
- joint_weight: bfloat16 [768, 1920], P(('wide', 'narrow')), may hold values from -0.21875 to 0.21875
- query_bias: bfloat16 [768], P(('wide', 'narrow')), may hold values from -6 to 6
- value_bias: bfloat16 [768], P(('wide', 'narrow')), may hold values from -4 to 4
- output_weight: bfloat16 [768, 768], P(('wide', 'narrow')), may hold values from -2.5 to 2.5
- output_bias: bfloat16 [768], P(('wide', 'narrow')), may hold values from -4 to 4
- feed_gain: bfloat16 [768], P(('wide', 'narrow')), may hold values from 0.5 to 1.5
- feed_shift: bfloat16 [768], P(('wide', 'narrow')), may hold values from -4 to 4
- expand_weight: bfloat16 [768, 3072], P(('wide', 'narrow')), may hold values from -0.21875 to 0.21875
- expand_bias: bfloat16 [3072], P(('wide', 'narrow')), may hold values from -4 to 4
- contract_weight: bfloat16 [3072, 768], P(('wide', 'narrow')), may hold values from -0.109375 to 0.109375
- contract_bias: bfloat16 [768], P(('wide', 'narrow')), may hold values from -4 to 4
Outputs:
- block_output: bfloat16 [32768, 768], P(('wide', 'narrow'))
- grad_tokens: bfloat16 [32768, 768], P(('wide', 'narrow'))
- grad_first_values: bfloat16 [32768, 384], P(('wide', 'narrow'))
- grad_attend_gain: float32 [768], P(('wide', 'narrow'))
- grad_attend_shift: float32 [768], P(('wide', 'narrow'))
- grad_joint_weight: float32 [768, 1920], P(('wide', 'narrow'))
- grad_query_bias: float32 [768], P(('wide', 'narrow'))
- grad_value_bias: float32 [768], P(('wide', 'narrow'))
- grad_output_weight: float32 [768, 768], P(('wide', 'narrow'))
- grad_output_bias: float32 [768], P(('wide', 'narrow'))
- grad_feed_gain: float32 [768], P(('wide', 'narrow'))
- grad_feed_shift: float32 [768], P(('wide', 'narrow'))
- grad_expand_weight: float32 [768, 3072], P(('wide', 'narrow'))
- grad_expand_bias: float32 [3072], P(('wide', 'narrow'))
- grad_contract_weight: float32 [3072, 768], P(('wide', 'narrow'))
- grad_contract_bias: float32 [768], P(('wide', 'narrow'))
All inputs are finite; a program needn't handle non-finite values.
Results may differ from a plain program's by a relative error of at most 0.012.
Values may be sent and summed in bfloat16 or wider, within the bound.
A program may use at most 256 MiB of HBM per device.

v0:
```python
import jax
import jax.numpy as jnp
from jax import lax
from jax.sharding import PartitionSpec as P

D = 768
HEADS = 12
HEAD = 64
LEN = 1024


epsilon = 1e-05


def layer_norm(values, gain, shift):
    center = values - jnp.mean(values, axis=-1, keepdims=True)
    spread = jnp.mean(center * center, axis=-1, keepdims=True)
    return center * lax.rsqrt(spread + epsilon) * gain + shift


def gelu_tanh(values):
    return jax.nn.gelu(values, approximate=True)


def causal_mask(block_index, block_rows, key_count):
    row_ids = block_index * block_rows + lax.broadcasted_iota(jnp.int32, (block_rows, key_count), 0)
    col_ids = lax.broadcasted_iota(jnp.int32, (block_rows, key_count), 1)
    return row_ids >= col_ids


def head_view(matrix, head_group):
    half_heads = HEADS // 2
    col_width = half_heads * HEAD
    return matrix[:, head_group * col_width : (head_group + 1) * col_width].reshape(
        matrix.shape[0], half_heads, HEAD
    )


def attend_forward(packed):
    queries, key_rows, value_rows = packed
    length = queries.shape[0]
    block_rows = min(512, length)
    score_scale = HEAD ** (-0.5)
    outputs = []
    log_totals = []
    for head_group in range(2):
        query_group = head_view(queries, head_group)
        key_group = head_view(key_rows, head_group)
        value_group = head_view(value_rows, head_group)
        group_out = []
        group_log = []
        for block_index in range(length // block_rows):
            finish = (block_index + 1) * block_rows
            scores = (
                jnp.einsum(
                    "qhd,khd->hqk",
                    query_group[finish - block_rows : finish],
                    key_group[:finish],
                    preferred_element_type=jnp.float32,
                )
                * score_scale
            )
            scores = jnp.where(causal_mask(block_index, block_rows, finish)[None], scores, -jnp.inf)
            row_peak = jnp.max(scores, axis=-1, keepdims=True)
            exponent = jnp.exp(scores - row_peak)
            row_total = jnp.sum(exponent, axis=-1, keepdims=True)
            weights_low = (exponent / row_total).astype(jnp.bfloat16)
            block_out = jnp.einsum(
                "hqk,khd->qhd",
                weights_low,
                value_group[:finish],
                preferred_element_type=jnp.float32,
            )
            group_out.append(block_out.reshape(block_rows, -1))
            group_log.append((row_peak + jnp.log(row_total))[..., 0])
        outputs.append(jnp.concatenate(group_out, axis=0))
        log_totals.append(jnp.concatenate(group_log, axis=1))
    return (jnp.concatenate(outputs, axis=1), jnp.concatenate(log_totals, axis=0))


def attend_backward(packed):
    queries, key_rows, value_rows, grad_mixed, log_total = packed
    length = queries.shape[0]
    block_rows = min(512, length)
    score_scale = HEAD ** (-0.5)
    half_heads = HEADS // 2
    grad_query_parts = []
    grad_key_parts = []
    grad_value_parts = []
    for head_group in range(2):
        query_group = head_view(queries, head_group)
        key_group = head_view(key_rows, head_group)
        value_group = head_view(value_rows, head_group)
        grad_group = head_view(grad_mixed, head_group)
        log_group = log_total[head_group * half_heads : (head_group + 1) * half_heads]
        key_accum = jnp.zeros(key_group.shape, jnp.float32)
        value_accum = jnp.zeros(value_group.shape, jnp.float32)
        query_blocks = []
        for block_index in range(length // block_rows):
            finish = (block_index + 1) * block_rows
            first_row = finish - block_rows
            query_block = query_group[first_row:finish]
            grad_block = grad_group[first_row:finish]
            scores = (
                jnp.einsum(
                    "qhd,khd->hqk",
                    query_block,
                    key_group[:finish],
                    preferred_element_type=jnp.float32,
                )
                * score_scale
            )
            scores = jnp.where(causal_mask(block_index, block_rows, finish)[None], scores, -jnp.inf)
            probs = jnp.exp(scores - log_group[:, first_row:finish, None])
            weights_low = probs.astype(jnp.bfloat16)
            grad_probs = jnp.einsum(
                "qhd,khd->hqk", grad_block, value_group[:finish], preferred_element_type=jnp.float32
            )
            inner_sum = jnp.sum(probs * grad_probs, axis=-1, keepdims=True)
            grad_scores = (probs * (grad_probs - inner_sum)).astype(jnp.bfloat16)
            query_blocks.append(
                jnp.einsum(
                    "hqk,khd->qhd",
                    grad_scores,
                    key_group[:finish],
                    preferred_element_type=jnp.float32,
                )
                * score_scale
            )
            key_accum = key_accum.at[:finish].add(
                jnp.einsum(
                    "hqk,qhd->khd", grad_scores, query_block, preferred_element_type=jnp.float32
                )
                * score_scale
            )
            value_accum = value_accum.at[:finish].add(
                jnp.einsum(
                    "hqk,qhd->khd", weights_low, grad_block, preferred_element_type=jnp.float32
                )
            )
        grad_query_parts.append(jnp.concatenate(query_blocks, axis=0).reshape(length, -1))
        grad_key_parts.append(key_accum.reshape(length, -1))
        grad_value_parts.append(value_accum.reshape(length, -1))
    return (
        jnp.concatenate(grad_query_parts, axis=1),
        jnp.concatenate(grad_key_parts, axis=1),
        jnp.concatenate(grad_value_parts, axis=1),
    )


def run_forward(tokens, first_values, attend_weights, feed_weights):
    attend_gain, attend_shift, joint_weight, query_bias, value_bias, output_weight, output_bias = (
        attend_weights
    )
    feed_gain, feed_shift, expand_weight, expand_bias, contract_weight, contract_bias = feed_weights
    token_count = tokens.shape[0]
    seq_count = token_count // LEN
    inputs_wide = tokens.astype(jnp.float32)
    hidden_one = layer_norm(
        inputs_wide, attend_gain.astype(jnp.float32), attend_shift.astype(jnp.float32)
    ).astype(jnp.bfloat16)
    projected = jnp.dot(hidden_one, joint_weight, preferred_element_type=jnp.float32)
    queries = (projected[:, :D] + query_bias.astype(jnp.float32)).astype(jnp.bfloat16)
    key_rows = projected[:, D : 2 * D].astype(jnp.bfloat16)
    value_rows = (
        jnp.concatenate([projected[:, 2 * D :], first_values.astype(jnp.float32)], axis=1)
        + value_bias.astype(jnp.float32)
    ).astype(jnp.bfloat16)
    mixed, log_total = lax.map(
        attend_forward,
        (
            queries.reshape(seq_count, LEN, D),
            key_rows.reshape(seq_count, LEN, D),
            value_rows.reshape(seq_count, LEN, D),
        ),
    )
    mixed_low = mixed.reshape(token_count, D).astype(jnp.bfloat16)
    resid = (
        inputs_wide
        + jnp.dot(mixed_low, output_weight, preferred_element_type=jnp.float32)
        + output_bias.astype(jnp.float32)
    )
    hidden_two = layer_norm(
        resid, feed_gain.astype(jnp.float32), feed_shift.astype(jnp.float32)
    ).astype(jnp.bfloat16)
    pre_act = jnp.dot(
        hidden_two, expand_weight, preferred_element_type=jnp.float32
    ) + expand_bias.astype(jnp.float32)
    activated = gelu_tanh(pre_act).astype(jnp.bfloat16)
    result = (
        resid
        + jnp.dot(activated, contract_weight, preferred_element_type=jnp.float32)
        + contract_bias.astype(jnp.float32)
    )
    return (
        inputs_wide,
        hidden_one,
        queries,
        key_rows,
        value_rows,
        log_total,
        mixed_low,
        resid,
        hidden_two,
        pre_act,
        activated,
        result,
    )


def body(
    tokens,
    first_values,
    cotangent,
    attend_gain,
    attend_shift,
    joint_weight,
    query_bias,
    value_bias,
    output_weight,
    output_bias,
    feed_gain,
    feed_shift,
    expand_weight,
    expand_bias,
    contract_weight,
    contract_bias,
):
    attend_shards = (
        attend_gain,
        attend_shift,
        joint_weight,
        query_bias,
        value_bias,
        output_weight,
        output_bias,
    )
    feed_shards = (
        feed_gain,
        feed_shift,
        expand_weight,
        expand_bias,
        contract_weight,
        contract_bias,
    )
    attend_full = (
        lax.all_gather(attend_gain, ("wide", "narrow"), axis=0, tiled=True),
        lax.all_gather(attend_shift, ("wide", "narrow"), axis=0, tiled=True),
        lax.all_gather(joint_weight, ("wide", "narrow"), axis=0, tiled=True),
        lax.all_gather(query_bias, ("wide", "narrow"), axis=0, tiled=True),
        lax.all_gather(value_bias, ("wide", "narrow"), axis=0, tiled=True),
        lax.all_gather(output_weight, ("wide", "narrow"), axis=0, tiled=True),
        lax.all_gather(output_bias, ("wide", "narrow"), axis=0, tiled=True),
    )
    feed_full = (
        lax.all_gather(feed_gain, ("wide", "narrow"), axis=0, tiled=True),
        lax.all_gather(feed_shift, ("wide", "narrow"), axis=0, tiled=True),
        lax.all_gather(expand_weight, ("wide", "narrow"), axis=0, tiled=True),
        lax.all_gather(expand_bias, ("wide", "narrow"), axis=0, tiled=True),
        lax.all_gather(contract_weight, ("wide", "narrow"), axis=0, tiled=True),
        lax.all_gather(contract_bias, ("wide", "narrow"), axis=0, tiled=True),
    )
    first_pass = run_forward(tokens, first_values, attend_full, feed_full)
    block_output = first_pass[-1].astype(jnp.bfloat16)
    feed_back = (
        lax.all_gather(feed_shards[0], ("wide", "narrow"), axis=0, tiled=True),
        lax.all_gather(feed_shards[1], ("wide", "narrow"), axis=0, tiled=True),
        lax.all_gather(feed_shards[2], ("wide", "narrow"), axis=0, tiled=True),
        lax.all_gather(feed_shards[3], ("wide", "narrow"), axis=0, tiled=True),
        lax.all_gather(feed_shards[4], ("wide", "narrow"), axis=0, tiled=True),
        lax.all_gather(feed_shards[5], ("wide", "narrow"), axis=0, tiled=True),
    )
    attend_back = (
        lax.all_gather(attend_shards[0], ("wide", "narrow"), axis=0, tiled=True),
        lax.all_gather(attend_shards[1], ("wide", "narrow"), axis=0, tiled=True),
        lax.all_gather(attend_shards[2], ("wide", "narrow"), axis=0, tiled=True),
        lax.all_gather(attend_shards[3], ("wide", "narrow"), axis=0, tiled=True),
        lax.all_gather(attend_shards[4], ("wide", "narrow"), axis=0, tiled=True),
        lax.all_gather(attend_shards[5], ("wide", "narrow"), axis=0, tiled=True),
        lax.all_gather(attend_shards[6], ("wide", "narrow"), axis=0, tiled=True),
    )
    (
        inputs_wide,
        hidden_one,
        queries,
        key_rows,
        value_rows,
        log_total,
        mixed_low,
        resid,
        hidden_two,
        pre_act,
        activated,
        unused_result,
    ) = run_forward(tokens, first_values, attend_back, feed_back)
    (
        back_gain_one,
        back_shift_one,
        back_joint,
        back_query_bias,
        back_value_bias,
        back_output,
        back_output_bias,
    ) = attend_back
    (
        back_gain_two,
        back_shift_two,
        back_expand,
        back_expand_bias,
        back_contract,
        back_contract_bias,
    ) = feed_back
    token_count = tokens.shape[0]
    seq_count = token_count // LEN
    grad_wide = cotangent.astype(jnp.float32)
    grad_contract = jnp.einsum(
        "nf,nd->fd", activated, cotangent, preferred_element_type=jnp.float32
    )
    grad_contract_bias = jnp.sum(grad_wide, axis=0)
    grad_act = jnp.einsum("nd,fd->nf", cotangent, back_contract, preferred_element_type=jnp.float32)
    gelu_pull = jax.vjp(gelu_tanh, pre_act)[1]
    grad_pre = gelu_pull(grad_act)[0].astype(jnp.bfloat16)
    grad_expand = jnp.einsum("nd,nf->df", hidden_two, grad_pre, preferred_element_type=jnp.float32)
    grad_expand_bias = jnp.sum(grad_pre.astype(jnp.float32), axis=0)
    grad_hidden_two = jnp.einsum(
        "nf,df->nd", grad_pre, back_expand, preferred_element_type=jnp.float32
    )
    norm_pull = jax.vjp(
        layer_norm, resid, back_gain_two.astype(jnp.float32), back_shift_two.astype(jnp.float32)
    )[1]
    grad_resid_norm, grad_feed_gain, grad_feed_shift = norm_pull(grad_hidden_two)
    grad_resid = grad_wide + grad_resid_norm
    feed_sums = (
        lax.psum_scatter(grad_feed_gain, ("wide", "narrow"), scatter_dimension=0, tiled=True),
        lax.psum_scatter(grad_feed_shift, ("wide", "narrow"), scatter_dimension=0, tiled=True),
        lax.psum_scatter(grad_expand, ("wide", "narrow"), scatter_dimension=0, tiled=True),
        lax.psum_scatter(grad_expand_bias, ("wide", "narrow"), scatter_dimension=0, tiled=True),
        lax.psum_scatter(grad_contract, ("wide", "narrow"), scatter_dimension=0, tiled=True),
        lax.psum_scatter(grad_contract_bias, ("wide", "narrow"), scatter_dimension=0, tiled=True),
    )
    grad_attn = grad_resid.astype(jnp.bfloat16)
    grad_output_bias = jnp.sum(grad_attn.astype(jnp.float32), axis=0)
    grad_output = jnp.einsum("nd,ne->de", mixed_low, grad_attn, preferred_element_type=jnp.float32)
    grad_mixed = jnp.einsum(
        "ne,de->nd", grad_attn, back_output, preferred_element_type=jnp.float32
    ).astype(jnp.bfloat16)
    grad_queries, grad_keys, grad_values = lax.map(
        attend_backward,
        (
            queries.reshape(seq_count, LEN, D),
            key_rows.reshape(seq_count, LEN, D),
            value_rows.reshape(seq_count, LEN, D),
            grad_mixed.reshape(seq_count, LEN, D),
            log_total,
        ),
    )
    grad_queries = grad_queries.reshape(token_count, D).astype(jnp.bfloat16)
    grad_keys = grad_keys.reshape(token_count, D).astype(jnp.bfloat16)
    grad_values = grad_values.reshape(token_count, D).astype(jnp.bfloat16)
    grad_query_bias = jnp.sum(grad_queries.astype(jnp.float32), axis=0)
    grad_value_bias = jnp.sum(grad_values.astype(jnp.float32), axis=0)
    grad_first_values = grad_values[:, D // 2 :]
    grad_projected = jnp.concatenate([grad_queries, grad_keys, grad_values[:, : D // 2]], axis=1)
    grad_joint = jnp.einsum(
        "nd,nc->dc", hidden_one, grad_projected, preferred_element_type=jnp.float32
    )
    grad_hidden_one = jnp.einsum(
        "nc,dc->nd", grad_projected, back_joint, preferred_element_type=jnp.float32
    )
    input_pull = jax.vjp(
        layer_norm,
        inputs_wide,
        back_gain_one.astype(jnp.float32),
        back_shift_one.astype(jnp.float32),
    )[1]
    grad_input_norm, grad_attend_gain, grad_attend_shift = input_pull(grad_hidden_one)
    grad_tokens = (grad_resid + grad_input_norm).astype(jnp.bfloat16)
    attend_sums = (
        lax.psum_scatter(grad_attend_gain, ("wide", "narrow"), scatter_dimension=0, tiled=True),
        lax.psum_scatter(grad_attend_shift, ("wide", "narrow"), scatter_dimension=0, tiled=True),
        lax.psum_scatter(grad_joint, ("wide", "narrow"), scatter_dimension=0, tiled=True),
        lax.psum_scatter(grad_query_bias, ("wide", "narrow"), scatter_dimension=0, tiled=True),
        lax.psum_scatter(grad_value_bias, ("wide", "narrow"), scatter_dimension=0, tiled=True),
        lax.psum_scatter(grad_output, ("wide", "narrow"), scatter_dimension=0, tiled=True),
        lax.psum_scatter(grad_output_bias, ("wide", "narrow"), scatter_dimension=0, tiled=True),
    )
    return (
        block_output,
        grad_tokens,
        grad_first_values,
        attend_sums[0],
        attend_sums[1],
        attend_sums[2],
        attend_sums[3],
        attend_sums[4],
        attend_sums[5],
        attend_sums[6],
        feed_sums[0],
        feed_sums[1],
        feed_sums[2],
        feed_sums[3],
        feed_sums[4],
        feed_sums[5],
    )


def solution(mesh):
    placed = (
        P(("wide", "narrow"), None),
        P(("wide", "narrow"), None),
        P(("wide", "narrow"), None),
        P(("wide", "narrow")),
        P(("wide", "narrow")),
        P(("wide", "narrow"), None),
        P(("wide", "narrow")),
        P(("wide", "narrow")),
        P(("wide", "narrow"), None),
        P(("wide", "narrow")),
        P(("wide", "narrow")),
        P(("wide", "narrow")),
        P(("wide", "narrow"), None),
        P(("wide", "narrow")),
        P(("wide", "narrow"), None),
        P(("wide", "narrow")),
    )
    return jax.shard_map(
        body,
        mesh=mesh,
        in_specs=placed,
        out_specs=(
            P(("wide", "narrow"), None),
            P(("wide", "narrow"), None),
            P(("wide", "narrow"), None),
            P(("wide", "narrow")),
            P(("wide", "narrow")),
            P(("wide", "narrow"), None),
            P(("wide", "narrow")),
            P(("wide", "narrow")),
            P(("wide", "narrow"), None),
            P(("wide", "narrow")),
            P(("wide", "narrow")),
            P(("wide", "narrow")),
            P(("wide", "narrow"), None),
            P(("wide", "narrow")),
            P(("wide", "narrow"), None),
            P(("wide", "narrow")),
        ),
        check_vma=False,
    )
```

profile of v0, /device:TPU:0, one launch (start us, length us, event | category | flops | bytes accessed | tf_op | source)
XLA Modules:
  0.0 814.6 jit_solution(18397408820010799597)
XLA Ops:
  18.4 42.7 %all-reduce.24 = (bf16[768]{0:T(1024)(128)(2,1)S(1)}, bf16[768]{0:T(1024)(128)(2,1)S(1)}, bf16[768]{0:T(1024)(128)(2,1)S(1)}, bf16[768]{0:T(1024)(128)(2,1)S(1)}...) all-reduce(bf16[768]{0:T(1024)(128)(2,1)S(1)} %dynamic-update-slice, ...), channel_id=1, replica_groups=mesh['wide'=8,'narrow'=4] {'wide','narrow'}, use_global_device_ids=true, to_apply=%add.8 | all-reduce | flops 9216 | bytes 36864
  72.6 7.9 fusion.95
  111.7 4.1 fusion.7
  127.6 5.0 fusion.66
  136.3 4.0 fusion.69
  140.3 4.0 fusion.68
  149.7 44.1 %all-gather.9.cloned.1.call-done = bf16[768,3072]{1,0:T(8,128)(2,1)} async-done(((bf16[24,3072]{1,0:T(8,128)(2,1)}), bf16[768,3072]{1,0:T(8,128)(2,1)}) %all-gather.9.cloned.1.call-update) | async-done | bytes 4718608 | tf_op jit(solution)/shard_map/all_gather | solution.py:258
  193.8 11.6 %fusion.85 = f32[1024,3072]{1,0:T(8,128)} fusion(bf16[768,3072]{1,0:T(8,128)(2,1)} %all-gather.9.cloned.1.call-done, f32[1024,768]{0,1:T(8,128)} %copy-done.7, f32[768]{0:T(1024)S(1)} %convert_element_type.173, f32[768]{0:T(1024)S(1)} %convert_element_type.172, f32[1024]{0:T(1024)S(1)} %fusion.77, f32[1024]{0:T(1024)S(1)} %broadcast_multiply_fusion), kind=kOutput, calls=%fused_computation.151 | convolution fusion | flops 4835770368 | bytes 20461568 | tf_op jit(solution)/shard_map/dot_general | solution.py:186
  205.4 53.5 %all-gather.11.cloned.1.call-done = bf16[3072,768]{1,0:T(8,128)(2,1)} async-done(((bf16[96,768]{1,0:T(8,128)(2,1)}), bf16[3072,768]{1,0:T(8,128)(2,1)}) %all-gather.11.cloned.1.call-update) | async-done | bytes 4718608 | tf_op jit(solution)/shard_map/all_gather | solution.py:260
  258.9 15.5 %convert_reduce_fusion = (f32[3072]{0:T(1024)}, bf16[1024,3072]{1,0:T(8,128)(2,1)S(1)}) fusion(f32[1024,3072]{1,0:T(8,128)} %fusion.85, f32[3072]{0:T(1024)S(1)} %copy-done.83, bf16[1024,768]{1,0:T(8,128)(2,1)S(1)} %copy-done.56, bf16[3072,768]{1,0:T(8,128)(2,1)} %all-gather.11.cloned.1.call-done), kind=kOutput, calls=%fused_computation.9 | convolution fusion | flops 4904186880 | bytes 25190400 | tf_op jit(solution)/shard_map/nd,fd->nf/dot_general | solution.py:320
  274.3 7.4 fusion.102
  281.7 3.9 copy.121
  306.6 6.9 multiply_reduce_fusion.2
  313.5 6.7 multiply_convert_fusion.3
  321.7 6.8 multiply_reduce_fusion.1
  328.5 10.3 %multiply_convert_fusion.1 = bf16[6,512,1024]{2,1,0:T(8,128)(2,1)} fusion(f32[6,512,1024]{2,1,0:T(8,128)} %get-tuple-element.349, f32[6,512,1024]{2,1,0:T(8,128)S(1)} %bitcast.129, f32[6,512]{1,0:T(8,128)S(1)} %get-tuple-element.348, f32[6,512]{1,0:T(8,128)S(1)} %log_add_fusion.2), kind=kLoop, calls=%fused_computation.13 | loop fusion | flops 12582912 | bytes 31481856 | tf_op jit(solution)/shard_map/while/body/eval_jaxpr/convert_element_type | solution.py:120
  338.7 5.1 fusion.73
  343.9 5.0 fusion.49
  350.8 7.5 multiply_reduce_fusion
  358.3 9.2 %multiply_convert_fusion = bf16[6,512,1024]{2,1,0:T(8,128)(2,1)} fusion(f32[6,512,1024]{2,1,0:T(8,128)} %get-tuple-element.353, f32[6,512,1024]{2,1,0:T(8,128)S(1)} %bitcast.125, f32[6,512]{1,0:T(8,128)S(1)} %get-tuple-element.352, f32[6,512]{1,0:T(8,128)S(1)} %log_add_fusion), kind=kLoop, calls=%fused_computation.10 | loop fusion | flops 12582912 | bytes 31481856 | tf_op jit(solution)/shard_map/while/body/eval_jaxpr/convert_element_type | solution.py:120
  367.5 5.2 fusion.72
  384.1 5.7 fusion.80
  389.8 13.4 %fusion.86 = f32[3072,768]{1,0:T(8,128)} fusion(bf16[1024,768]{1,0:T(8,128)(2,1)} %param.42, f32[1024,3072]{1,0:T(8,128)} %fusion.85, f32[3072]{0:T(1024)S(1)} %copy-done.83), kind=kOutput, calls=%fused_computation.152 | convolution fusion | flops 4863295488 | bytes 23605248 | tf_op jit(solution)/shard_map/nf,nd->fd/dot_general | solution.py:316
  403.3 10.7 %fusion.84 = f32[768,3072]{1,0:T(8,128)} fusion(bf16[1024,3072]{1,0:T(8,128)(2,1)} %copy-done.97, f32[1024,768]{0,1:T(8,128)} %copy-done.7, f32[768]{0:T(1024)S(1)} %convert_element_type.173, f32[768]{0:T(1024)S(1)} %convert_element_type.172, f32[1024]{0:T(1024)S(1)} %fusion.77, f32[1024]{0:T(1024)S(1)} %broadcast_multiply_fusion), kind=kOutput, calls=%fused_computation.150 | convolution fusion | flops 4835770368 | bytes 18888704 | tf_op jit(solution)/shard_map/nd,nf->df/dot_general | solution.py:323
  414.6 12.6 %add_convert_fusion.1 = bf16[1024,768]{0,1:T(8,128)(2,1)} fusion(f32[1024,768]{0,1:T(8,128)} %copy-done.7, bf16[3072,768]{1,0:T(8,128)(2,1)} %all-gather.11.cloned.1.call-done, f32[768]{0:T(1024)S(1)} %convert_element_type.177, f32[1024,3072]{1,0:T(8,128)} %fusion.85, f32[3072]{0:T(1024)S(1)} %copy-done.83), kind=kOutput, calls=%fused_computation.82 | convolution fusion | flops 4865654784 | bytes 22035456 | tf_op jit(solution)/shard_map/dot_general | solution.py:192
  429.8 4.2 fusion.57
  433.9 6.3 fusion.46
  441.5 8.4 %fusion.101 = (f32[768]{0:T(1024)S(1)}, f32[1024,768]{1,0:T(8,128)}) fusion(bf16[1024,1920]{0,1:T(8,128)(2,1)} %copy-done.61, bf16[768,1920]{1,0:T(8,128)(2,1)} %all-gather.5.cloned.1.call-done), kind=kOutput, calls=%fused_computation.166 | convolution fusion | flops 3020684544 | bytes 10030080 | tf_op jit(solution)/shard_map/nc,dc->nd/dot_general | solution.py:367
  461.3 41.9 %all-reduce.23 = (f32[768]{0:T(1024)S(1)}, f32[768]{0:T(1024)S(1)}, f32[768]{0:T(1024)S(1)}, f32[768]{0:T(1024)S(1)}, f32[768]{0:T(1024)S(1)}, /*index=5*/f32[76...) all-reduce(f32[768]{0:T(1024)S(1)} %get-tuple-element.294, ...), channel_id=2, replica_groups=mesh['wide'=8,'narrow'=4] {'wide','narrow'}, use_global_device_ids=true, to_apply=%region_21.22.clone | all-reduce | flops 9216 | bytes 73728
  509.9 14.4 %reduce-scatter.13.cloned.1.call-done = f32[24,1920]{1,0:T(8,128)} async-done(((f32[768,1920]{1,0:T(8,128)}), f32[24,1920]{1,0:T(8,128)}) %reduce-scatter.13.cloned.1.call-update) | async-done | bytes 184336
  524.3 142.4 %reduce-scatter.11.cloned.1.call-done = f32[96,768]{1,0:T(8,128)} async-done(((f32[3072,768]{1,0:T(8,128)}), f32[96,768]{1,0:T(8,128)}) %reduce-scatter.11.cloned.1.call-update) | async-done | bytes 294928 | tf_op jit(solution)/shard_map/reduce_scatter | solution.py:338
  666.7 140.9 %reduce-scatter.9.cloned.1.call-done = f32[24,3072]{1,0:T(8,128)} async-done(((f32[768,3072]{1,0:T(8,128)}), f32[24,3072]{1,0:T(8,128)}) %reduce-scatter.9.cloned.1.call-update) | async-done | bytes 294928 | tf_op jit(solution)/shard_map/reduce_scatter | solution.py:336
  (379 shorter events, 131.9 us)
Async XLA Ops:
  7.2 65.4 %all-gather.5.cloned.1.call-start = ((), (), s32[]{:S(2)}) async-start(), calls=%async_computation.4 | async-start | bytes 3041280 | tf_op jit(solution)/shard_map/all_gather | solution.py:249
  7.9 136.4 %all-gather.7.cloned.1.call-start = ((), (), s32[]{:S(2)}) async-start(), calls=%async_computation.5 | async-start | bytes 1216512 | tf_op jit(solution)/shard_map/all_gather | solution.py:252
  8.7 185.1 %all-gather.9.cloned.1.call-start = ((), (), s32[]{:S(2)}) async-start(), calls=%async_computation.6 | async-start | bytes 4866048 | tf_op jit(solution)/shard_map/all_gather | solution.py:258
  9.4 249.5 %all-gather.11.cloned.1.call-start = ((), (), s32[]{:S(2)}) async-start(), calls=%async_computation.7 | async-start | bytes 4866048 | tf_op jit(solution)/shard_map/all_gather | solution.py:260
  10.0 500.0 %reduce-scatter.7.cloned.1.call-start = ((), (), s32[]{:S(2)}) async-start(), calls=%async_computation.8 | async-start | bytes 2433024 | tf_op jit(solution)/shard_map/reduce_scatter | solution.py:384
  61.6 11.0 %copy-start.75 = (f32[768]{0:T(1024)}, f32[768]{0:T(1024)S(1)}, u32[]{:S(2)}) copy-start(f32[768]{0:T(1024)S(1)} %convert_element_type.159) | copy-start | bytes 9220
  61.6 11.0 %copy-start.85 = (f32[768]{0:T(1024)}, f32[768]{0:T(1024)S(1)}, u32[]{:S(2)}) copy-start(f32[768]{0:T(1024)S(1)} %convert_element_type.160) | copy-start | bytes 9220
  65.3 7.4 copy-start.4
  66.0 14.5 %copy-start.77 = (f32[1024]{0:T(1024)}, f32[1024]{0:T(1024)S(1)}, u32[]{:S(2)}) copy-start(f32[1024]{0:T(1024)S(1)} %fusion.32) | copy-start | bytes 12292
  66.1 14.5 %copy-start.79 = (f32[1024]{0:T(1024)}, f32[1024]{0:T(1024)S(1)}, u32[]{:S(2)}) copy-start(f32[1024]{0:T(1024)S(1)} %fusion.76) | copy-start | bytes 12292
  82.7 26.7 %copy-start.24 = (bf16[1024,384]{0,1:T(8,128)(2,1)}, bf16[1024,384]{0,1:T(8,128)(2,1)S(1)}, u32[]{:S(2)}) copy-start(bf16[1024,384]{0,1:T(8,128)(2,1)S(1)} %copy.111) | copy-start | bytes 2359300
  87.3 29.1 %copy-start.23 = (bf16[1024,384]{0,1:T(8,128)(2,1)}, bf16[1024,384]{0,1:T(8,128)(2,1)S(1)}, u32[]{:S(2)}) copy-start(bf16[1024,384]{0,1:T(8,128)(2,1)S(1)} %copy.118) | copy-start | bytes 2359300
  95.5 20.9 %copy-start.28 = (bf16[512,384]{0,1:T(8,128)(2,1)}, bf16[512,384]{0,1:T(8,128)(2,1)S(1)}, u32[]{:S(2)}) copy-start(bf16[512,384]{0,1:T(8,128)(2,1)S(1)} %copy.117) | copy-start | bytes 1179652
  127.5 12.7 %copy-start.46 = (bf16[1024,384]{0,1:T(8,128)(2,1)}, bf16[1024,384]{0,1:T(8,128)(2,1)S(1)}, u32[]{:S(2)}) copy-start(bf16[1024,384]{0,1:T(8,128)(2,1)S(1)} %copy.116) | copy-start | bytes 2359300
  127.6 7.1 slice-start.6
  132.7 7.5 slice-start
  149.6 109.2 %copy-start.56 = (bf16[1024,768]{1,0:T(8,128)(2,1)S(1)}, bf16[1024,768]{1,0:T(8,128)(2,1)}, u32[]{:S(2)}) copy-start(bf16[1024,768]{1,0:T(8,128)(2,1)} %param.42) | copy-start | bytes 4718596
  149.7 109.2 %copy-start.83 = (f32[3072]{0:T(1024)S(1)}, f32[3072]{0:T(1024)}, u32[]{:S(2)}) copy-start(f32[3072]{0:T(1024)} %convert_element_type.175) | copy-start | bytes 36868
  258.9 15.5 %copy-start.26 = (bf16[768,3072]{1,0:T(8,128)(2,1)S(1)}, bf16[768,3072]{1,0:T(8,128)(2,1)}, u32[]{:S(2)}) copy-start(bf16[768,3072]{1,0:T(8,128)(2,1)} %all-gather.9.cloned.1.call-done) | copy-start | bytes 14155780
  274.3 7.4 copy-start.97
  306.5 217.9 %reduce-scatter.13.cloned.1.call-start = ((), (), s32[]{:S(2)}) async-start(), calls=%async_computation.11 | async-start | bytes 6082560
  306.5 15.1 %slice-start.9 = ((s8[12582912]{0:T(1024)(128)(4,1)}), s8[4194304]{0:T(1024)(128)(4,1)S(1)}, s32[]{:S(2)}) async-start(s8[12582912]{0:T(1024)(128)(4,1)} %bitcast.128), calls=%async_computation.21 | async-start | bytes 8388608
  306.5 15.1 %slice-start.10 = ((s8[12582912]{0:T(1024)(128)(4,1)}), s8[4194304]{0:T(1024)(128)(4,1)S(1)}, s32[]{:S(2)}) async-start(s8[12582912]{0:T(1024)(128)(4,1)} %bitcast.128), calls=%async_computation.22 | async-start | bytes 8388608
  313.5 8.2 %slice-start.11 = ((s8[12582912]{0:T(1024)(128)(4,1)}), s8[4194304]{0:T(1024)(128)(4,1)S(1)}, s32[]{:S(2)}) async-start(s8[12582912]{0:T(1024)(128)(4,1)} %bitcast.128), calls=%async_computation.23 | async-start | bytes 8388608
  328.5 10.3 %copy-start.25 = (bf16[1024,384]{0,1:T(8,128)(2,1)S(1)}, bf16[1024,384]{0,1:T(8,128)(2,1)}, u32[]{:S(2)}) copy-start(bf16[1024,384]{0,1:T(8,128)(2,1)} %copy-done.24) | copy-start | bytes 2359300
  328.5 22.4 %slice-start.3 = ((s8[12582912]{0:T(1024)(128)(4,1)}), s8[4194304]{0:T(1024)(128)(4,1)S(1)}, s32[]{:S(2)}) async-start(s8[12582912]{0:T(1024)(128)(4,1)} %bitcast.124), calls=%async_computation.15 | async-start | bytes 8388608
  328.5 22.4 %slice-start.4 = ((s8[12582912]{0:T(1024)(128)(4,1)}), s8[4194304]{0:T(1024)(128)(4,1)S(1)}, s32[]{:S(2)}) async-start(s8[12582912]{0:T(1024)(128)(4,1)} %bitcast.124), calls=%async_computation.16 | async-start | bytes 8388608
  338.7 12.1 %slice-start.5 = ((s8[12582912]{0:T(1024)(128)(4,1)}), s8[4194304]{0:T(1024)(128)(4,1)S(1)}, s32[]{:S(2)}) async-start(s8[12582912]{0:T(1024)(128)(4,1)} %bitcast.124), calls=%async_computation.17 | async-start | bytes 8388608
  367.5 7.3 slice-start.18
  389.8 276.9 %reduce-scatter.11.cloned.1.call-start = ((), (), s32[]{:S(2)}) async-start(), calls=%async_computation.10 | async-start | bytes 9732096 | tf_op jit(solution)/shard_map/reduce_scatter | solution.py:338
  403.2 404.3 %reduce-scatter.9.cloned.1.call-start = ((), (), s32[]{:S(2)}) async-start(), calls=%async_computation.9 | async-start | bytes 9732096 | tf_op jit(solution)/shard_map/reduce_scatter | solution.py:336
  440.3 9.6 %copy-start.21 = (bf16[1024,6,64]{0,2,1:T(8,128)(2,1)}, bf16[1024,6,64]{0,2,1:T(8,128)(2,1)S(1)}, u32[]{:S(2)}) copy-start(bf16[1024,6,64]{0,2,1:T(8,128)(2,1)S(1)} %fusion.46) | copy-start | bytes 2359300
  (94 other events, 315.2 us)
Sparse Core Ops, SparseCore 0:
  10.9 61.7 all-gather.4
  75.4 52.9 all-gather.6
  131.2 62.5 all-gather.8
  196.5 62.3 all-gather.10
  306.6 97.8 reduce-scatter.6
  411.5 112.7 reduce-scatter.12
  531.8 134.8 reduce-scatter.10
  673.2 134.3 reduce-scatter.8
where the time goes:
time: 821 us; the launch traced here: 815 us
  waiting for transfers between devices  402 us (49%)
  matrix products  183 us (22%)
  blocking collectives  84.5 us (10%)
  local copies, waits for them, and re-layouts  69.1 us (8%)
  other arithmetic  60.4 us (7%)
  between operations  15.7 us (2%)
    reduce_scatter x1, waiting for transfers between devices, body(): lax.psum_scatter(grad_contract, ('wide', 'narrow'), scatter_dimension=0,...  142 us
    reduce_scatter x1, waiting for transfers between devices, body(): lax.psum_scatter(grad_expand, ('wide', 'narrow'), scatter_dimension=0, ti...  141 us
    unnamed x2, blocking collectives  84.5 us
    all_gather x1, waiting for transfers between devices, body(): lax.all_gather(contract_weight, ('wide', 'narrow'), axis=0, tiled=True)  53.5 us
    all_gather x1, waiting for transfers between devices, body(): lax.all_gather(expand_weight, ('wide', 'narrow'), axis=0, tiled=True)  44.1 us
    unnamed x272, local copies, waits for them, and re-layouts  38.4 us
    convert_element_type x4, other arithmetic, attend_backward(): grad_scores = (probs * (grad_probs - inner_sum)).astype(jnp.bfloat16)  27.9 us
    dot_general x4, matrix products, attend_backward(): jnp.einsum('qhd,khd->hqk', grad_block, value_group[:finish], preferred_el...  22.7 us
  transfers between devices with their start and end apart: 8, of which 6 were waited for; matrix products, arithmetic and copies ran while one was open for 31% of the time, Pallas kernels for 0%

commit v1 on v0

v1 whole, which is shorter than its diff:
```python
import functools

import jax
import jax.numpy as jnp
from jax import lax
from jax.experimental import pallas as pl
from jax.experimental.pallas import tpu as pltpu
from jax.sharding import PartitionSpec as P

D = 768
HEAD = 64
FF = 3072
LEN = 1024
HALF = D // 2
SLAB = D // 8
PAIRS = D // (2 * HEAD)
QB = 256
EPS = 1e-05
BF = jnp.bfloat16
F32 = jnp.float32
MESH = pl.DeviceIdType.MESH
AXES = ("wide", "narrow")

UNITS = 15
JOINT_COLS = (0, 768, 1536, 384, 1152)
GAIN1, SHIFT1, QBIAS, VBIAS, OBIAS, GAIN2, SHIFT2, CBIAS, EBIAS = range(9)
VROWS = 16


def dot(left, right, left_dim=1, right_dim=0):
    return lax.dot_general(left, right, (((left_dim,), (right_dim,)), ((), ())), preferred_element_type=F32)


def loop(count, step):
    lax.fori_loop(0, count, lambda i, c: (step(i), c)[1], 0)


def rows_of(index, size):
    return pl.ds(pl.multiple_of(index * size, size), size)


def norm_parts(values):
    center = values - jnp.mean(values, axis=-1, keepdims=True)
    inv = lax.rsqrt(jnp.mean(center * center, axis=-1, keepdims=True) + EPS)
    return center * inv, inv


def norm_back(values, grad, gain):
    unit, inv = norm_parts(values)
    scaled = grad * gain
    mean_one = jnp.mean(scaled, axis=-1, keepdims=True)
    mean_two = jnp.mean(scaled * unit, axis=-1, keepdims=True)
    grad_in = inv * (scaled - mean_one - unit * mean_two)
    return grad_in, jnp.sum(grad * unit, axis=0, keepdims=True), jnp.sum(grad, axis=0, keepdims=True)


class Nothing:
    def __getattr__(self, name):
        return lambda *a, **k: None


def two_units(ref, unit):
    return jnp.concatenate([ref[unit].reshape(D, HALF), ref[unit + 1].reshape(D, HALF)], axis=1)


def stages(r, comm):
    vec = r.vec

    def vrow(i):
        return vec[i : i + 1, :]

    order = []

    def stage(function):
        order.append(function)
        return function


    def norm_one(i):
        rows = rows_of(i, 128)
        unit, _ = norm_parts(r.tokens[rows, :].astype(F32))
        r.h1[rows, :] = (unit * vrow(GAIN1) + vrow(SHIFT1)).astype(BF)

    @stage
    def run_norm_one():
        loop(LEN // 128, norm_one)


    def project_a(i):
        rows = rows_of(i, 512)
        weights = jnp.concatenate([r.wall[u].reshape(D, HALF) for u in (0, 1, 2)], axis=1)
        out = dot(r.h1[rows, :], weights)
        r.q[rows, 0:HALF] = ((out[:, 0:HALF] + vec[QBIAS : QBIAS + 1, 0:HALF]).astype(BF) * HEAD ** (-0.5)).astype(BF)
        r.k[rows, 0:HALF] = out[:, HALF:D].astype(BF)
        r.v[rows, 0:HALF] = (out[:, D:] + vec[VBIAS : VBIAS + 1, 0:HALF]).astype(BF)

    @stage
    def run_project_a():
        loop(LEN // 512, project_a)

    def project_b(i):
        rows = rows_of(i, 512)
        out = dot(r.h1[rows, :], two_units(r.wall, 3))
        r.q[rows, HALF:D] = ((out[:, 0:HALF] + vec[QBIAS : QBIAS + 1, HALF:D]).astype(BF) * HEAD ** (-0.5)).astype(BF)
        r.k[rows, HALF:D] = out[:, HALF:D].astype(BF)
        r.v[rows, HALF:D] = (r.v[rows, HALF:D].astype(F32) + vec[VBIAS : VBIAS + 1, HALF:D]).astype(BF)

    lanes = lax.broadcasted_iota(jnp.int32, (QB, 128), 1)
    first_lanes = lanes < HEAD
    lane_row = lax.broadcasted_iota(jnp.int32, (1, 128), 1)
    head_mask = [(lane_row < HEAD).astype(F32).astype(BF), (lane_row >= HEAD).astype(F32).astype(BF)]
    tri = lax.broadcasted_iota(jnp.int32, (QB, QB), 0) >= lax.broadcasted_iota(jnp.int32, (QB, QB), 1)

    def attend(pair):
        cols = rows_of(pair, 128)
        for block in range(LEN // QB):
            first, finish = block * QB, (block + 1) * QB
            qp = r.q[first:finish, cols]
            outs = []
            logs = r.logs[first:finish, :]
            for h in range(2):
                scores = dot(qp * head_mask[h], r.k[0:finish, cols], 1, 1)
                diag = jnp.where(tri, scores[:, first:finish], -jnp.inf)
                scores = diag if block == 0 else jnp.concatenate([scores[:, :first], diag], axis=1)
                peak = jnp.max(scores, axis=-1, keepdims=True)
                raised = jnp.exp(scores - peak)
                total = jnp.sum(raised, axis=-1, keepdims=True)
                outs.append(dot(raised.astype(BF), r.v[0:finish, cols]) * (1.0 / total))
                logs = jnp.where(lanes == 2 * pair + h, peak + jnp.log(total), logs)
            r.logs[first:finish, :] = logs
            r.mixed[first:finish, cols] = jnp.where(first_lanes, outs[0], outs[1]).astype(BF)

    @stage
    def run_attend():
        def step(i):
            @pl.when(i == PAIRS // 2)
            def _():
                comm.before("project_b")
                loop(LEN // 512, project_b)

            attend(i)
            comm.tick("attend", i)

        loop(PAIRS, step)

    def out_project(i):
        rows = rows_of(i, 256)
        resid = r.tokens[rows, :].astype(F32) + dot(r.mixed[rows, :], two_units(r.wall, 5)) + vrow(OBIAS)
        r.resid[rows, :] = resid
        unit, _ = norm_parts(resid)
        r.tokens[rows, :] = (unit * vrow(GAIN2) + vrow(SHIFT2)).astype(BF)

    @stage
    def run_out_project():
        loop(LEN // 256, out_project)
    h2 = r.tokens

    alpha = 0.7978845608028654
    beta = alpha * 0.044715

    def expand(j):
        comm.tick("expand", j)
        cols = rows_of(j, D)
        bias = vec[pl.ds(EBIAS + j, 1), :]

        def step(i):
            rows = rows_of(i, 256)
            pre = dot(h2[rows, :], two_units(r.wall, 7 + 2 * j)) + bias
            square = pre * pre
            bent = jnp.tanh(pre * (alpha + beta * square))
            half = 0.5 * bent + 0.5
            slope = half + (pre * (0.5 - 0.5 * bent * bent)) * (alpha + (3.0 * beta) * square)
            r.act[rows, cols] = (pre * half).astype(BF)
            r.gp[rows, cols] = slope.astype(BF)

        loop(LEN // 256, step)

    @stage
    def run_expand():
        loop(4, expand)

    def grad_contract(w):
        y, x, c = w // 4, (w // 2) % 2, w % 2
        grad = dot(r.act[:, rows_of(w, HALF)], r.cot[...], 0, 0)
        r.gc[0, y, x, c] = grad[:, :HALF].astype(BF)
        r.gc[1, y, x, c] = grad[:, HALF:].astype(BF)
        comm.tick("grad_contract", w)

    @stage
    def run_grad_contract():
        loop(8, grad_contract)

    def column_sum(i, total):
        return total + jnp.sum(r.cot[rows_of(i, 128), :].astype(F32), axis=0, keepdims=True)

    @stage
    def run_contract_bias():
        r.gvec[...] = jnp.zeros_like(r.gvec)
        r.gvec[CBIAS : CBIAS + 1, :] = lax.fori_loop(0, LEN // 128, column_sum, jnp.zeros((1, D), F32))

    def block_out(i):
        rows = rows_of(i, 256)
        weights = jnp.concatenate([r.wc[0].reshape(FF, HALF), r.wc[1].reshape(FF, HALF)], axis=1)
        r.leaving[rows, :] = (r.resid[rows, :] + dot(r.act[rows, :], weights) + vrow(CBIAS)).astype(BF)
        comm.tick("block_out", i)

    @stage
    def run_block_out():
        loop(LEN // 256, block_out)

    def grad_pre(j):
        y, x = j // 2, j % 2
        cols = rows_of(j, D)
        sums = jnp.zeros((1, D), F32)

        def step(i, sums):
            rows = rows_of(i, 512)
            weights = jnp.concatenate([r.wc[0, y, x].reshape(D, HALF), r.wc[1, y, x].reshape(D, HALF)], axis=1)
            grad = (dot(r.cot[rows, :], weights, 1, 1) * r.gp[rows, cols].astype(F32)).astype(BF)
            r.gp[rows, cols] = grad
            return sums + jnp.sum(grad.astype(F32), axis=0, keepdims=True)

        r.gvec[pl.ds(EBIAS + j, 1), :] = lax.fori_loop(0, LEN // 512, step, sums)
        comm.tick("grad_pre", j)

    @stage
    def run_grad_pre():
        loop(4, grad_pre)

    def grad_expand(j):
        grad = dot(h2[...], r.gp[:, rows_of(j, D)], 0, 0).astype(BF)
        for side in range(2):
            part = grad[:, side * HALF : (side + 1) * HALF].reshape(2, 2, 2, SLAB, HALF)
            r.ge[j // 2, :, :, :, rows_of(2 * (j % 2) + side, SLAB), :] = part
        comm.tick("grad_expand", j)

    @stage
    def run_grad_expand():
        loop(4, grad_expand)

    def grad_norm_two(i, sums):
        rows = rows_of(i, 256)
        weights = jnp.concatenate([r.wall[u].reshape(D, HALF) for u in range(7, 15)], axis=1)
        grad_in, gain, shift = norm_back(r.resid[rows, :], dot(r.gp[rows, :], weights, 1, 1), vrow(GAIN2))
        grad = r.cot[rows, :].astype(F32) + grad_in
        low = grad.astype(BF)
        r.resid[rows, :] = grad
        r.tokens[rows, :] = low
        comm.tick("grad_norm_two", i)
        return sums[0] + gain, sums[1] + shift, sums[2] + jnp.sum(low.astype(F32), axis=0, keepdims=True)

    @stage
    def run_grad_norm_two():
        zero = jnp.zeros((1, D), F32)
        gain, shift, obias = lax.fori_loop(0, LEN // 256, grad_norm_two, (zero, zero, zero))
        r.gvec[GAIN2 : GAIN2 + 1, :] = gain
        r.gvec[SHIFT2 : SHIFT2 + 1, :] = shift
        r.gvec[OBIAS : OBIAS + 1, :] = obias
    gattn = r.tokens

    def grad_output(i):
        grad = dot(r.mixed[:, rows_of(i, HALF)], gattn[...], 0, 0).astype(BF)
        for side in range(2):
            r.wall[12 + side, i] = grad[:, side * HALF : (side + 1) * HALF].reshape(2, 2, SLAB, HALF)

    @stage
    def run_grad_output():
        loop(2, grad_output)

    def grad_mixed(i):
        rows = rows_of(i, 512)
        grad = dot(gattn[rows, :], two_units(r.wall, 5), 1, 1).astype(BF)
        r.cot[rows, :] = grad

    @stage
    def run_grad_mixed():
        loop(LEN // 512, grad_mixed)

    def attend_back(pair):
        cols = rows_of(pair, 128)
        qsum = jnp.zeros((1, 128), F32)
        for block in reversed(range(LEN // QB)):
            first, finish = block * QB, (block + 1) * QB
            qp = r.q[first:finish, cols]
            gm = r.cot[first:finish, cols]
            kp = r.k[0:finish, cols]
            vp = r.v[0:finish, cols]
            logs = r.logs[first:finish, :]
            inner = gm.astype(F32) * r.mixed[first:finish, cols].astype(F32)
            parts = []
            for h in range(2):
                qm, gh = qp * head_mask[h], gm * head_mask[h]
                log_total = jnp.sum(jnp.where(lanes == 2 * pair + h, logs, 0.0), axis=-1, keepdims=True)
                mine = first_lanes if h == 0 else jnp.logical_not(first_lanes)
                inner_sum = jnp.sum(jnp.where(mine, inner, 0.0), axis=-1, keepdims=True)
                probs = jnp.exp(dot(qm, kp, 1, 1) - log_total)
                diag = jnp.where(tri, probs[:, first:finish], 0.0)
                probs = diag if block == 0 else jnp.concatenate([probs[:, :first], diag], axis=1)
                grad_scores = (probs * (dot(gh, vp, 1, 1) - inner_sum)).astype(BF)
                parts.append((probs.astype(BF), grad_scores, qm, gh, dot(grad_scores, kp)))
            gq = (jnp.where(first_lanes, parts[0][4], parts[1][4]) * HEAD ** (-0.5)).astype(BF)
            r.act[first:finish, cols] = gq
            qsum = qsum + jnp.sum(gq.astype(F32), axis=0, keepdims=True)
            both = [jnp.concatenate([a, b], axis=0) for a, b in zip(parts[0][:4], parts[1][:4])]
            gk = dot(both[1], both[2], 0, 0)
            gv = dot(both[0], both[3], 0, 0)
            if finish == LEN:
                r.gk[...] = gk
                r.gv[...] = gv
            else:
                r.gk[0:finish, :] += gk
                r.gv[0:finish, :] += gv
        low = r.gv[...].astype(BF)
        r.act[:, rows_of(PAIRS + pair, 128)] = r.gk[...].astype(BF)
        r.act[:, rows_of(2 * PAIRS + pair, 128)] = low
        r.gvec[QBIAS : QBIAS + 1, cols] = qsum
        r.gvec[VBIAS : VBIAS + 1, cols] = jnp.sum(low.astype(F32), axis=0, keepdims=True)

    def grad_joint(unit):
        start = JOINT_COLS[unit]
        grad = dot(r.h1[...], r.act[:, start : start + HALF], 0, 0).astype(BF)
        r.wall[7 + unit] = grad.reshape(2, 2, 2, SLAB, HALF)

    @stage
    def run_attend_back():
        def step(i):
            attend_back(i)

            @pl.when(i == PAIRS // 2 - 1)
            def _():
                for unit in (0, 1, 2):
                    grad_joint(unit)

            comm.tick("attend_back", i)

        loop(PAIRS, step)

    @stage
    def run_grad_joint():
        for unit in (3, 4):
            grad_joint(unit)

    def grad_norm_one(i, sums):
        rows = rows_of(i, 256)
        weights = jnp.concatenate([r.wall[u].reshape(D, HALF) for u in (0, 3, 1, 4, 2)], axis=1)
        grad_hidden = dot(r.act[rows, 0 : 2 * D + HALF], weights, 1, 1)
        grad_in, gain, shift = norm_back(r.mixed[rows, :].astype(F32), grad_hidden, vrow(GAIN1))
        r.leaving[rows, :] = (r.resid[rows, :] + grad_in).astype(BF)
        comm.tick("grad_norm_one", i)
        return sums[0] + gain, sums[1] + shift

    @stage
    def run_grad_norm_one():
        zero = jnp.zeros((1, D), F32)
        gain, shift = lax.fori_loop(0, LEN // 256, grad_norm_one, (zero, zero))
        r.gvec[GAIN1 : GAIN1 + 1, :] = gain
        r.gvec[SHIFT1 : SHIFT1 + 1, :] = shift
    return order


def compute(r, comm):
    comm.start()
    for run in stages(r, comm):
        name = run.__name__.removeprefix("run_")
        comm.before(name)
        run()
        comm.after(name)
    comm.finish()


class Refs:
    def __init__(self, **refs):
        self.__dict__.update(refs)


STATE = dict(
    tokens=((LEN, D), BF),
    cot=((LEN, D), BF),
    wall=((UNITS, 2, 2, 2, SLAB, HALF), BF),
    wc=((2, 2, 2, 2, FF // 8, HALF), BF),
    vec=((VROWS, D), F32),
    gvec=((VROWS, D), F32),
    h1=((LEN, D), BF),
    q=((LEN, D), BF),
    k=((LEN, D), BF),
    v=((LEN, D), BF),
    mixed=((LEN, D), BF),
    logs=((LEN, 128), F32),
    resid=((LEN, D), F32),
    leaving=((LEN, D), BF),
    act=((LEN, FF), BF),
    gp=((LEN, FF), BF),
    gc=((2, 2, 2, 2, FF // 8, HALF), BF),
    gk=((LEN, 128), F32),
    gv=((LEN, 128), F32),
)
ANY = pl.BlockSpec(memory_space=pl.ANY)
VMEM = pl.BlockSpec(memory_space=pltpu.VMEM)


class Whole(Nothing):
    def __init__(self, r, sem):
        self.r, self.sem = r, sem

    def move(self, source, target):
        copy = pltpu.make_async_copy(source, target, self.sem)
        copy.start()
        copy.wait()

    def start(self):
        r = self.r
        for source, target in (
            (r.tokens_in, r.tokens), (r.first_in, r.v.at[:, HALF:D]), (r.cot_in, r.cot),
            (r.wall_in, r.wall), (r.wc_in, r.wc), (r.vec_in, r.vec),
        ):
            self.move(source, target)

    def before(self, what):
        if what == "grad_norm_one":
            self.move(self.r.tokens_in, self.r.mixed)

    def after(self, what):
        r = self.r
        if what == "block_out":
            self.move(r.leaving, r.block_output)
        elif what == "grad_norm_one":
            self.move(r.leaving, r.grad_tokens)
        elif what == "grad_contract":
            self.move(r.gc, r.gc_out)
        elif what == "grad_expand":
            self.move(r.ge, r.ge_out)
        elif what == "grad_output":
            self.move(r.wall.at[12:14], r.gjo_out.at[5:7])
        elif what == "grad_joint":
            self.move(r.wall.at[7:12], r.gjo_out.at[0:5])
            self.move(r.act.at[:, 2 * D + HALF : 3 * D], r.grad_first)

    def finish(self):
        self.move(self.r.gvec, self.r.gvec_out)


def whole_kernel(*refs):
    names = ["tokens_in", "first_in", "cot_in", "wall_in", "wc_in", "vec_in"]
    names += ["block_output", "grad_tokens", "grad_first", "gc_out", "ge_out", "gjo_out", "gvec_out"]
    names += list(STATE) + ["sem"]
    r = Refs(**dict(zip(names, refs)))
    r.ge = r.wc
    compute(r, Whole(r, r.sem))


def units_of(matrix):
    count = matrix.shape[1] // HALF
    return matrix.reshape(2, 2, 2, SLAB, count, HALF).transpose(4, 0, 1, 2, 3, 5)


def matrix_of(units):
    count = units.shape[0]
    return units.transpose(1, 2, 3, 4, 0, 5).reshape(D, count * HALF)


def outside(args):
    (tokens, first_values, cotangent, gain1, shift1, joint, qbias, vbias, output, obias,
     gain2, shift2, expand, ebias, contract, cbias) = args
    gather = functools.partial(lax.all_gather, axis_name=AXES, axis=0, tiled=True)
    scatter = functools.partial(lax.psum_scatter, axis_name=AXES, scatter_dimension=0, tiled=True)
    joint_units = units_of(gather(joint))
    wall = jnp.concatenate(
        [jnp.stack([joint_units[start // HALF] for start in JOINT_COLS]), units_of(gather(output)), units_of(gather(expand))]
    )
    wc = gather(contract).reshape(2, 2, 2, FF // 8, 2, HALF).transpose(4, 0, 1, 2, 3, 5)
    vec = jnp.stack([gather(v) for v in (gain1, shift1, qbias, vbias, obias, gain2, shift2, cbias)])
    vec = jnp.concatenate([vec, gather(ebias).reshape(4, D), jnp.zeros((4, D), BF)]).astype(F32)
    sds = jax.ShapeDtypeStruct
    block_output, grad_tokens, grad_first, gc, ge, gjo, gvec = pl.pallas_call(
        whole_kernel,
        out_shape=(
            sds((LEN, D), BF), sds((LEN, D), BF), sds((LEN, HALF), BF), sds(wc.shape, BF), sds(wc.shape, BF),
            sds((7,) + wall.shape[1:], BF), sds((VROWS, D), F32),
        ),
        in_specs=[ANY] * 6,
        out_specs=(ANY,) * 7,
        scratch_shapes=[pltpu.VMEM(*item) for item in STATE.values()] + [pltpu.SemaphoreType.DMA],
        compiler_params=pltpu.CompilerParams(vmem_limit_bytes=64 * 2**20),
    )(tokens, first_values, cotangent, wall, wc, vec)
    gc = gc.transpose(1, 2, 3, 4, 0, 5).reshape(FF, D).astype(F32)
    ge = ge.reshape(2, 8, 4, SLAB, HALF).transpose(1, 3, 0, 2, 4).reshape(D, FF).astype(F32)
    order = [JOINT_COLS.index(start * HALF) for start in range(5)]
    gj = jnp.concatenate([matrix_of(gjo[u : u + 1]) for u in order], axis=1).astype(F32)
    go = matrix_of(gjo[5:7]).astype(F32)
    small = [scatter(gvec[i]) for i in range(8)]
    return (
        block_output, grad_tokens, grad_first, small[GAIN1], small[SHIFT1], scatter(gj), small[QBIAS], small[VBIAS],
        scatter(go), small[OBIAS], small[GAIN2], small[SHIFT2], scatter(ge), scatter(gvec[8:12].reshape(FF)),
        scatter(gc), small[CBIAS],
    )


class Linked:
    def __init__(self, r, depth):
        self.r, self.depth = r, depth
        wide, self.mz = lax.axis_index("wide"), lax.axis_index("narrow")
        self.my, self.mx, self.mc = wide // 4, (wide // 2) % 2, wide % 2
        self.wide = wide
        self.peer = {
            "c": (wide + 1 - 2 * self.mc, self.mz),
            "x": (wide + 2 - 4 * self.mx, self.mz),
            "y": (wide + 4 - 8 * self.my, self.mz),
        }
        for d in range(1, depth):
            self.peer["z%d" % d] = (wide, lax.rem(self.mz + d, depth))
        self.far = [lax.rem(self.mz + d, depth) for d in range(depth)]

    def remote(self, source, target, sems, place, where):
        send, recv = sems
        return pltpu.make_async_remote_copy(
            src_ref=source, dst_ref=target, send_sem=send.at[place], recv_sem=recv.at[place],
            device_id=self.peer[where], device_id_type=MESH,
        )

    def gather_z(self, g):
        r, mz, out = self.r, self.mz, []
        for d in range(1, self.depth):
            where = "z%d" % d
            if g in ("C0", "C1"):
                h = int(g[1])
                parts = [(
                    r.wc_in.at[:, h * HALF : (h + 1) * HALF],
                    r.wc.at[h, self.my, self.mx, self.mc, rows_of(mz, SLAB), :],
                )]
            else:
                source, stage, spans = self.small(g)
                parts = [(source.at[:, a:b], stage.at[mz, :, a:b]) for a, b in spans]
            for part, (source, target) in enumerate(parts):
                out.append(self.remote(source, target, (r.gz_send, r.gz_recv), (GROUPS.index(g), d - 1, part), where))
        return out

    def small(self, g):
        r = self.r
        if g[0] == "J":
            return r.wj_in, r.sj, [(c, c + HALF) for c in (JOINT_COLS[0:3] if g == "J0" else JOINT_COLS[3:5])]
        if g[0] == "O":
            return r.wo_in, r.so, [(0, D)]
        j = int(g[1])
        return r.we_in, r.se, [(j * D, (j + 1) * D)]

    def assemble(self, g):
        r = self.r
        if g in ("C0", "C1"):
            h = int(g[1])
            r.wc[h, self.my, self.mx, self.mc, rows_of(self.mz, SLAB), :] = r.wc_in[:, h * HALF : (h + 1) * HALF]
            return
        source, stage, spans = self.small(g)
        unit = UNIT_SPAN[g][0]
        for a, b in spans:
            stage[self.mz, :, a:b] = source[:, a:b]
            for c in range(a, b, HALF):
                rows = jnp.concatenate([stage[z, :, c : c + HALF].astype(F32) for z in range(self.depth)], axis=0)
                r.wall[unit, self.my, self.mx, self.mc] = rows.astype(BF)
                unit += 1

    def views(self, g):
        if g[0] == "C":
            return self.r.wc, (int(g[1]),), pl.ds(0, FF // 16), pl.ds(FF // 16, FF // 16)
        a, b = UNIT_SPAN[g]
        return self.r.wall, (pl.ds(a, b - a),), pl.ds(0, SLAB // 2), pl.ds(SLAB // 2, SLAB // 2)

    def gather_copies(self, g, step):
        ref, lead, low, high = self.views(g)
        y, x, c, both = self.my, self.mx, self.mc, slice(None)
        if step == 1:
            plan = [((y, x, c, low), "x", 0), ((y, x, c, high), "y", 1)]
        elif step == 2:
            plan = [((y, both, c, low), "y", 2), ((both, x, c, high), "x", 3)]
        else:
            plan = [((both, both, c), "c", 4)]
        sems = (self.r.g_send, self.r.g_recv)
        return [self.remote(ref.at[lead + at], ref.at[lead + at], sems, (GROUPS.index(g), n), w) for at, w, n in plan]

    def gather(self, g, step):
        if step == 0:
            for copy in self.gather_z(g):
                copy.start()
            return
        if step == 1:
            for copy in self.gather_z(g):
                copy.wait_recv()
            self.assemble(g)
        else:
            for copy in self.gather_copies(g, step - 1):
                copy.wait_recv()
        if step < 4:
            for copy in self.gather_copies(g, step):
                copy.start()
        else:
            for copy in self.gather_z(g) + [c for n in (1, 2, 3) for c in self.gather_copies(g, n)]:
                copy.wait_send()

    def vec_copies(self, way, step):
        r = self.r
        held, got = ((r.vsum, r.vgot), (r.gvec, r.ggot))[way]
        order = ("z", "x", "y", "c") if way == 0 else ("c", "x", "y", "z")
        kind = order[step]
        wheres = ["z%d" % d for d in range(1, self.depth)] if kind == "z" else [kind]
        out = []
        for where in wheres:
            n = {"c": 0, "x": 1, "y": 2}[kind] if kind != "z" else 2 + int(where[1])
            out.append(self.remote(held, got.at[n], (r.v_send, r.v_recv), (way, n), where))
        return out

    def vec_step(self, way, step):
        r = self.r
        held, got = ((r.vsum, r.vgot), (r.gvec, r.ggot))[way]
        if step > 0:
            copies = self.vec_copies(way, step - 1)
            for copy in copies:
                copy.wait()
            total = held[...].astype(F32)
            order = ("z", "x", "y", "c") if way == 0 else ("c", "x", "y", "z")
            kind = order[step - 1]
            places = [2 + d for d in range(1, self.depth)] if kind == "z" else [{"c": 0, "x": 1, "y": 2}[kind]]
            for n in places:
                total = total + got[n].astype(F32)
            if way == 0 and step == 4:
                r.vec[...] = total
            else:
                held[...] = total.astype(held.dtype)
        if step < 4:
            for copy in self.vec_copies(way, step):
                copy.start()

    def big(self, g):
        return g[0] in "CE"

    def grad_ref(self, g):
        if self.big(g):
            rows = FF // 8
            return self.r.gc if g[0] == "C" else self.r.ge, (int(g[1]),), pl.ds(0, rows // 2), pl.ds(rows // 2, rows // 2)
        a, b = GRAD_SPAN[g]
        return self.r.wall, (pl.ds(a, b - a),), pl.ds(0, SLAB // 2), pl.ds(SLAB // 2, SLAB // 2)

    def got_ref(self, g):
        r = self.r
        if self.big(g):
            return r.big_core, r.big_one, r.big_two, (int(g[1]),)
        a, b = GRAD_SPAN[g]
        return r.small_core, r.small_one, r.small_two, (pl.ds(a - 7, b - a),)

    def scatter_copies(self, g, step):
        ref, lead, low, high = self.grad_ref(g)
        core, one, two, mine = self.got_ref(g)
        y, x, c, both = self.my, self.mx, self.mc, slice(None)
        r, index = self.r, SUMS.index(g)
        if step == 0:
            plan = [((both, both, 1 - c), core.at[mine], "c", 0)]
        elif step == 1:
            plan = [
                ((both, 1 - x, c, low), one.at[0].at[mine], "x", 1),
                ((1 - y, both, c, high), one.at[1].at[mine], "y", 2),
            ]
        elif step == 2:
            plan = [
                ((1 - y, x, c, low), two.at[0].at[mine], "y", 3),
                ((y, 1 - x, c, high), two.at[1].at[mine], "x", 4),
            ]
        else:
            out = []
            for d in range(1, self.depth):
                far = self.far[d]
                if g[0] == "C":
                    parts = [(ref.at[lead + (y, x, c, rows_of(far, SLAB))], r.zc.at[int(g[1]), d - 1])]
                else:
                    stage, got, spans = self.stage(g)
                    parts = [(stage.at[far, :, a:b], got.at[d - 1, :, a:b]) for a, b in spans]
                for part, (source, target) in enumerate(parts):
                    place = (index, d - 1, part)
                    out.append(self.remote(source, target, (r.sz_send, r.sz_recv), place, "z%d" % d))
            return out
        sems = (r.s_send, r.s_recv)
        return [self.remote(ref.at[lead + at], target, sems, (index, n), w) for at, target, w, n in plan]

    def stage(self, g):
        r = self.r
        if g[0] == "J":
            return r.sj, r.zj, [(c, c + HALF) for c in (JOINT_COLS[0:3] if g == "J0" else JOINT_COLS[3:5])]
        if g[0] == "O":
            return r.so, r.zo, [(0, D)]
        h = int(g[1])
        return r.se, r.ze, [(h * 2 * D, (h + 1) * 2 * D)]

    def scatter(self, g, step):
        r = self.r
        ref, lead, low, high = self.grad_ref(g)
        core, one, two, _ = self.got_ref(g)
        y, x, c = self.my, self.mx, self.mc
        if step > 0:
            for copy in self.scatter_copies(g, step - 1):
                copy.wait_recv()

        def add(at, got):
            ref[at] = (ref[at].astype(F32) + got.astype(F32)).astype(BF)

        if self.big(g):
            leads = [(lead[0], lead[0])]
        else:
            a, b = GRAD_SPAN[g]
            leads = [(u, u - 7) for u in range(a, b)]
        if step == 1:
            for u, v in leads:
                def both_add(i, u=u, v=v):
                    add((u, i // 2, i % 2, c), core[v, i // 2, i % 2])

                loop(4, both_add)
        elif step == 2:
            for u, v in leads:
                def one_add(i, u=u, v=v):
                    add((u, i, x, c, low), one[0, v, i])
                    add((u, y, i, c, high), one[1, v, i])

                loop(2, one_add)
        elif step == 3:
            for n, (u, v) in enumerate(leads):
                if g[0] == "C":
                    add((u, y, x, c, low), two[0, v])
                    add((u, y, x, c, high), two[1, v])
                    continue
                final = jnp.concatenate(
                    [
                        ref[u, y, x, c, low, :].astype(F32) + two[0, v].astype(F32),
                        ref[u, y, x, c, high, :].astype(F32) + two[1, v].astype(F32),
                    ],
                    axis=0,
                )
                stage, _, spans = self.stage(g)
                starts = [s for a, b in spans for s in range(a, b, HALF)]
                share = SLAB // self.depth
                count = final.shape[0] // SLAB
                for s in range(count):
                    start = starts[n * count + s]
                    for z in range(self.depth):
                        rows = final[s * SLAB + z * share : s * SLAB + (z + 1) * share]
                        stage[z, :, start : start + HALF] = rows.astype(BF)
        elif step == 4:
            if g[0] == "C":
                h = int(g[1])
                total = r.gc[h, y, x, c, rows_of(self.mz, SLAB), :].astype(F32)
                for d in range(self.depth - 1):
                    total = total + r.zc[h, d].astype(F32)
                r.gc_out[:, h * HALF : (h + 1) * HALF] = total
            else:
                stage, got, spans = self.stage(g)
                out = {"J": r.gj_out, "O": r.go_out, "E": r.ge_out}[g[0]]
                for a, b in spans:
                    total = stage[self.mz, :, a:b].astype(F32)
                    for d in range(self.depth - 1):
                        total = total + got[d, :, a:b].astype(F32)
                    out[:, a:b] = total
            for n in range(4):
                for copy in self.scatter_copies(g, n):
                    copy.wait_send()
        turns = ([], [(0, "c")], [(1, "x"), (2, "y")], [(3, "y"), (4, "x")], [])
        if g[0] == "C":
            for n, where in turns[step]:
                pl.semaphore_signal(
                    r.free_sem.at[n, lead[0]], inc=1, device_id=self.peer[where], device_id_type=MESH
                )
        if g[0] == "E" and step < 3:
            for n, _ in turns[step + 1]:
                pl.semaphore_wait(r.free_sem.at[n, lead[0]], 1)
        if step < 4:
            for copy in self.scatter_copies(g, step):
                copy.start()

    def run(self, words):
        for word in words:
            name, step = word.split(".")
            if name == "vec":
                self.vec_step(0, int(step))
            elif name == "gvec":
                self.vec_step(1, int(step))
            elif name[0] == "g":
                self.gather(name[1:], int(step))
            elif name[0] == "s":
                self.scatter(name[1:], int(step))
            else:
                self.local(int(step)).wait()

    def local(self, n):
        r = self.r
        source, target = (
            (r.tokens_in, r.tokens),
            (r.first_in, r.v.at[:, HALF:D]),
            (r.cot_in, r.cot),
            (r.tokens_in, r.mixed),
            (r.act.at[:, 2 * D + HALF : 3 * D], r.grad_first),
            (r.leaving, r.block_output),
            (r.leaving, r.grad_tokens),
        )[n]
        return pltpu.make_async_copy(source, target, r.local_sem.at[n])

    def start(self):
        r = self.r
        for n in range(3):
            self.local(n).start()
        r.vsum[...] = r.vec_in[...]
        barrier = pltpu.get_barrier_semaphore()
        for where in self.peer:
            pl.semaphore_signal(barrier, inc=1, device_id=self.peer[where], device_id_type=MESH)
        pl.semaphore_wait(barrier, len(self.peer))
        self.run(PLAN["start"])

    def before(self, what):
        self.run(PLAN.get("before " + what, ()))

    def after(self, what):
        if what == "attend_back":
            self.local(3).start()
            self.local(4).start()
        elif what == "block_out":
            self.local(5).start()
        elif what == "grad_norm_one":
            self.local(6).start()
        self.run(PLAN.get("after " + what, ()))

    def tick(self, what, i):
        for n in range(8):
            words = PLAN.get("%s %d" % (what, n), ())
            if words:
                @pl.when(i == n)
                def _(words=words):
                    self.run(words)

    def finish(self):
        self.run(PLAN["finish"])


UNIT_SPAN = dict(J0=(0, 3), J1=(3, 5), O0=(5, 7), E0=(7, 9), E1=(9, 11), E2=(11, 13), E3=(13, 15))
GROUPS = ("J0", "J1", "O0", "E0", "E1", "E2", "E3", "C0", "C1")
GRAD_SPAN = dict(J0=(7, 10), J1=(10, 12), O0=(12, 14))
BIG = ("C0", "C1", "E0", "E1")
SUMS = BIG + ("O0", "J0", "J1")
PLAN = {
    "start": ("vec.0", "gJ0.0", "local.0", "vec.1", "gJ0.1", "gJ1.0", "gO0.0", "gE0.0", "gE1.0", "vec.2", "gJ0.2", "gE2.0", "gE3.0", "vec.3", "gJ1.1", "gC0.0", "gC1.0", "gJ0.3", "vec.4", "gO0.1",),
    "before project_a": ("gJ1.2", "gJ0.4",),
    "after project_a": ("gJ1.3", "gO0.2", "gE0.1", "local.1",),
    "attend 0": ("gE1.1",),
    "attend 1": ("gJ1.4", "gO0.3", "gE0.2",),
    "attend 2": ("gE2.1",),
    "attend 3": ("gE0.3", "gE1.2",),
    "attend 4": ("gE3.1", "gO0.4",),
    "attend 5": ("gE1.3", "gE2.2", "gC0.1",),
    "after out_project": ("gE0.4", "gE3.2", "gC1.1",),
    "expand 1": ("gE1.4", "gE2.3",),
    "expand 2": ("gE2.4", "gE3.3", "gC0.2",),
    "expand 3": ("gE3.4",),
    "before grad_contract": ("local.2",),
    "grad_contract 5": ("gC1.2", "gC0.3",),
    "after contract_bias": ("sC0.0", "sC1.0", "gC0.4", "gC1.3", "gC1.4",),
    "block_out 2": ("sC0.1",),
    "after block_out": ("sC1.1",),
    "grad_pre 3": ("sC0.2",),
    "grad_expand 1": ("sE0.0",),
    "after grad_expand": ("sE1.0", "sC1.2",),
    "grad_norm_two 2": ("sE0.1", "sC0.3",),
    "after grad_norm_two": ("sE1.1",),
    "after grad_output": ("sO0.0", "sC1.3",),
    "after grad_mixed": ("sE0.2", "sO0.1",),
    "attend_back 0": ("sE1.2", "sC0.4",),
    "attend_back 1": ("sE0.3", "sO0.2", "sC1.4",),
    "attend_back 2": ("sE1.3", "sJ0.0",),
    "attend_back 3": ("sJ0.1", "sO0.3", "sE0.4",),
    "attend_back 4": ("sE1.4", "sO0.4",),
    "attend_back 5": ("sJ0.2",),
    "after grad_joint": ("sJ1.0", "sJ0.3",),
    "before grad_norm_one": ("local.3", "local.4", "local.5",),
    "grad_norm_one 0": ("sJ1.1",),
    "grad_norm_one 2": ("sJ1.2",),
    "after grad_norm_one": ("gvec.0", "sJ1.3", "sJ0.4", "gvec.1", "gvec.2", "gvec.3",),
    "finish": ("sJ1.4", "gvec.4", "local.6",),
}


def linked_scratch(depth):
    share = SLAB // depth
    far = max(depth - 1, 1)
    dma = pltpu.SemaphoreType.DMA
    return dict(
        sj=pltpu.VMEM((depth, share, 2 * D + HALF), BF),
        so=pltpu.VMEM((depth, share, D), BF),
        se=pltpu.VMEM((depth, share, FF), BF),
        zj=pltpu.VMEM((far, share, 2 * D + HALF), BF),
        zo=pltpu.VMEM((far, share, D), BF),
        ze=pltpu.VMEM((far, share, FF), BF),
        zc=pltpu.VMEM((2, far, FF // 8 // depth, HALF), BF),
        big_core=pltpu.VMEM((2, 2, 2, FF // 8, HALF), BF),
        big_one=pltpu.VMEM((2, 2, 2, FF // 16, HALF), BF),
        big_two=pltpu.VMEM((2, 2, FF // 16, HALF), BF),
        small_core=pltpu.VMEM((7, 2, 2, SLAB, HALF), BF),
        small_one=pltpu.VMEM((2, 7, 2, SLAB // 2, HALF), BF),
        small_two=pltpu.VMEM((2, 7, SLAB // 2, HALF), BF),
        vsum=pltpu.VMEM((VROWS, D), BF),
        vgot=pltpu.VMEM((2 + depth, VROWS, D), BF),
        ggot=pltpu.VMEM((2 + depth, VROWS, D), F32),
        gz_send=dma((9, far, 3)), gz_recv=dma((9, far, 3)), g_send=dma((9, 5)), g_recv=dma((9, 5)),
        sz_send=dma((7, far, 3)), sz_recv=dma((7, far, 3)), s_send=dma((7, 5)), s_recv=dma((7, 5)),
        v_send=dma((2, 2 + depth)), v_recv=dma((2, 2 + depth)), local_sem=dma((7,)), free_sem=pltpu.SemaphoreType.REGULAR((5, 2)),
    )


def linked_kernel(depth, *refs):
    names = ["tokens_in", "first_in", "cot_in", "wj_in", "wo_in", "we_in", "wc_in", "vec_in"]
    names += ["block_output", "grad_tokens", "grad_first", "gj_out", "go_out", "ge_out", "gc_out", "gvec_out"]
    names += list(STATE) + list(linked_scratch(depth))
    r = Refs(**dict(zip(names, refs)))
    r.ge = r.wc
    compute(r, Linked(r, depth))
    r.gvec_out[...] = r.gvec[...]


def linked(depth, args):
    (tokens, first_values, cotangent, gain1, shift1, joint, qbias, vbias, output, obias,
     gain2, shift2, expand, ebias, contract, cbias) = args
    count = 8 * depth
    share = D // count
    me = lax.axis_index("wide") * depth + lax.axis_index("narrow")
    own = jnp.tile(jnp.stack([gain1, shift1, qbias, vbias, obias, gain2, shift2, cbias]), (1, count))
    place = lax.broadcasted_iota(jnp.int32, (8, D), 1)
    own = jnp.where(place // share == me, own, jnp.zeros((), BF))
    wide_bias = jnp.tile(ebias, count).reshape(4, D)
    place = lax.broadcasted_iota(jnp.int32, (4, D), 0) * D + lax.broadcasted_iota(jnp.int32, (4, D), 1)
    wide_bias = jnp.where(place // (4 * share) == me, wide_bias, jnp.zeros((), BF))
    vec = jnp.concatenate([own, wide_bias, jnp.zeros((VROWS - 12, D), BF)])
    sds = jax.ShapeDtypeStruct
    block_output, grad_tokens, grad_first, gj, go, ge, gc, gvec = pl.pallas_call(
        functools.partial(linked_kernel, depth),
        out_shape=(
            sds((LEN, D), BF), sds((LEN, D), BF), sds((LEN, HALF), BF), sds(joint.shape, F32), sds(output.shape, F32),
            sds(expand.shape, F32), sds(contract.shape, F32), sds((VROWS, D), F32),
        ),
        in_specs=[ANY] * 3 + [VMEM] * 5,
        out_specs=(ANY, ANY, ANY, VMEM, VMEM, VMEM, VMEM, VMEM),
        scratch_shapes=[pltpu.VMEM(*item) for item in STATE.values()] + list(linked_scratch(depth).values()),
        compiler_params=pltpu.CompilerParams(
            vmem_limit_bytes=64 * 2**20, collective_id=0, has_side_effects=True
        ),
    )(tokens, first_values, cotangent, joint, output, expand, contract, vec)
    small = lax.dynamic_slice(gvec, (0, me * share), (8, share))
    grad_ebias = lax.dynamic_slice(gvec[8:12].reshape(FF), (me * 4 * share,), (4 * share,))
    return (
        block_output, grad_tokens, grad_first, small[GAIN1], small[SHIFT1], gj, small[QBIAS], small[VBIAS],
        go, small[OBIAS], small[GAIN2], small[SHIFT2], ge, grad_ebias, gc, small[CBIAS],
    )


def solution(mesh):
    split, flat = P(AXES, None), P(AXES)
    wide, depth = mesh.shape["wide"], mesh.shape["narrow"]
    if wide == 8 and SLAB % (8 * depth) == 0:
        body = lambda *args: linked(depth, args)
    else:
        body = lambda *args: outside(args)
    return jax.shard_map(
        body,
        mesh=mesh,
        in_specs=(split, split, split, flat, flat, split, flat, flat, split, flat, flat, flat, split, flat, split, flat),
        out_specs=(split, split, split, flat, flat, split, flat, flat, split, flat, flat, flat, split, flat, split, flat),
        check_vma=False,
    )
```

time: 821 us -> 201 us (0.24)
  waiting for transfers between devices: 402 us -> 0 us
  Pallas kernels: 0 us -> 187 us
  matrix products: 183 us -> 0 us
  blocking collectives: 84.5 us -> 0 us
  other arithmetic: 60.4 us -> 0.75 us
  local copies, waits for them, and re-layouts: 69.1 us -> 12.6 us
  between operations: 15.7 us -> 0.7 us
    reduce_scatter x3 -> x0, waiting for transfers between devices: 283 us -> none  [the longest x1 142 us: body(): lax.psum_scatter(grad_contract, ('wide', 'narrow'), scatter_dimension=0,...]
    pallas_call x0 -> x1, Pallas kernels: none -> 187 us  [linked(): pl.pallas_call(functools.partial(linked_kernel, depth), out_shape=(sds((L...]
    dot_general x36 -> x0, matrix products: 183 us -> none  [the longest x4 22.7 us: attend_backward(): jnp.einsum('qhd,khd->hqk', grad_block, value_group[:finish], preferred_el...]
    all_gather x4 -> x0, waiting for transfers between devices: 101 us -> none  [the longest x1 53.5 us: body(): lax.all_gather(contract_weight, ('wide', 'narrow'), axis=0, tiled=True)]
    unnamed x2 -> x0, blocking collectives: 84.5 us -> none
    convert_element_type x16 -> x0, other arithmetic: 34.2 us -> none  [the longest x4 27.9 us: attend_backward(): grad_scores = (probs * (grad_probs - inner_sum)).astype(jnp.bfloat16)]
    unnamed x272 -> x19, local copies, waits for them, and re-layouts: 38.4 us -> 8.25 us
    reduce_sum x14 -> x0, other arithmetic: 24 us -> none  [the longest x4 10.4 us: attend_forward(): row_total = jnp.sum(exponent, axis=-1, keepdims=True)]
  transfers between devices with their start and end apart: 8 -> 0, of which waited for: 6 -> 0; matrix products, arithmetic and copies ran while one was open for 31% -> 0% of each run, Pallas kernels for 0% -> 0%
where the time goes in v1:
time: 201 us
  Pallas kernels  187 us (93%)
  local copies, waits for them, and re-layouts  12.6 us (6%)
    pallas_call x1, Pallas kernels, linked(): pl.pallas_call(functools.partial(linked_kernel, depth), out_shape=(sds((L...  187 us
    unnamed x19, local copies, waits for them, and re-layouts  8.25 us

profile of v1, /device:TPU:0, one launch (start us, length us, event | category | flops | bytes accessed | tf_op | source)
XLA Modules:
  0.0 200.6 jit_solution(6513152472405592790)
XLA Ops:
  0.7 0.8 stack.35
  1.5 0.1 tile.20
  1.6 0.7 tile.21
  2.3 0.1 tile.22
  2.4 0.1 fusion.3
  2.5 0.6 pad_maximum_fusion.refs_7_
  3.1 186.6 %shard_map.279 = (bf16[1024,768]{1,0:T(8,128)(2,1)}, bf16[1024,768]{1,0:T(8,128)(2,1)}, bf16[1024,384]{1,0:T(8,128)(2,1)}, f32[24,1920]{1,0:T(8,128)}, f32[24,76...) custom-call(bf16[1024,768]{1,0:T(8,128)(2,1)} %refs_0_.1, bf16[1024,384]{1,0:T(8,128)(2,1)} %refs_1_.1, ...), custom_call_target="tpu_custom_call" | custom-call | tf_op jit(solution)/shard_map/pallas_call | solution.py:933
  189.7 0.8 constant_dynamic-slice_fusion
  190.5 0.5 slice_bitcast_fusion
  191.0 0.7 slice.34
  191.8 0.6 dynamic_slice.7
  192.4 0.0 copy-start
  192.4 2.8 %copy.39 = bf16[1024,768]{1,0:T(8,128)(2,1)} copy(bf16[1024,768]{1,0:T(8,128)(2,1)} %get-tuple-element.58) | data formatting | bytes 3145728
  195.2 0.0 copy-done
  195.2 0.0 copy-start.1
  195.2 1.1 copy.40
  196.3 0.5 copy-done.1
  196.8 0.0 copy-start.4
  196.8 0.0 copy-start.5
  196.8 0.0 copy-start.3
  196.8 0.0 copy-start.2
  196.8 0.9 copy.41
  197.7 0.2 copy-done.4
  197.9 0.7 copy.42
  198.6 0.0 copy-done.5
  198.6 0.6 copy.43
  199.2 0.0 copy-done.3
  199.2 0.7 copy.44
  199.9 0.0 copy-done.2
  199.9 0.7 copy.45
  (7 shorter events, 0.1 us)
Async XLA Ops:
  192.4 2.8 %copy-start = (bf16[1024,768]{1,0:T(8,128)(2,1)S(1)}, bf16[1024,768]{1,0:T(8,128)(2,1)}, u32[]{:S(2)}) copy-start(bf16[1024,768]{1,0:T(8,128)(2,1)} %get-tuple-element.59) | copy-start | bytes 4718596
  195.2 1.7 copy-start.1
  196.8 1.1 copy-start.4
  196.8 1.7 copy-start.5
  196.8 2.4 %copy-start.3 = (f32[24,3072]{1,0:T(8,128)S(1)}, f32[24,3072]{1,0:T(8,128)}, u32[]{:S(2)}) copy-start(f32[24,3072]{1,0:T(8,128)} %get-tuple-element.70) | copy-start | bytes 884740
  196.8 3.1 %copy-start.2 = (f32[96,768]{1,0:T(8,128)S(1)}, f32[96,768]{1,0:T(8,128)}, u32[]{:S(2)}) copy-start(f32[96,768]{1,0:T(8,128)} %get-tuple-element.72) | copy-start | bytes 884740

commit v2 on v1

v2 whole, which is shorter than its diff:
```python
import functools

import jax
import jax.numpy as jnp
from jax import lax
from jax.experimental import pallas as pl
from jax.experimental.pallas import tpu as pltpu
from jax.sharding import PartitionSpec as P

D = 768
HEAD = 64
FF = 3072
LEN = 1024
HALF = D // 2
SLAB = D // 8
PAIRS = D // (2 * HEAD)
QB = 256
EPS = 1e-05
BF = jnp.bfloat16
F32 = jnp.float32
MESH = pl.DeviceIdType.MESH
AXES = ("wide", "narrow")

UNITS = 15
JOINT_COLS = (0, 768, 1536, 384, 1152)
GAIN1, SHIFT1, QBIAS, VBIAS, OBIAS, GAIN2, SHIFT2, CBIAS, EBIAS = range(9)
VROWS = 16
G_GAIN1, G_SHIFT1 = 0, 1
G_QBIAS, G_VBIAS, G_OBIAS, G_GAIN2, G_SHIFT2, G_CBIAS = range(8, 14)
G_EBIAS = 16
GROWS = 24


def dot(left, right, left_dim=1, right_dim=0):
    return lax.dot_general(left, right, (((left_dim,), (right_dim,)), ((), ())), preferred_element_type=F32)


def loop(count, step):
    lax.fori_loop(0, count, lambda i, c: (step(i), c)[1], 0)


def rows_of(index, size):
    return pl.ds(pl.multiple_of(index * size, size), size)


def norm_parts(values):
    center = values - jnp.mean(values, axis=-1, keepdims=True)
    inv = lax.rsqrt(jnp.mean(center * center, axis=-1, keepdims=True) + EPS)
    return center * inv, inv


def norm_back(values, grad, gain):
    unit, inv = norm_parts(values)
    scaled = grad * gain
    mean_one = jnp.mean(scaled, axis=-1, keepdims=True)
    mean_two = jnp.mean(scaled * unit, axis=-1, keepdims=True)
    grad_in = inv * (scaled - mean_one - unit * mean_two)
    return grad_in, jnp.sum(grad * unit, axis=0, keepdims=True), jnp.sum(grad, axis=0, keepdims=True)


class Nothing:
    def __getattr__(self, name):
        return lambda *a, **k: None


def two_units(ref, unit):
    return jnp.concatenate([ref[unit].reshape(D, HALF), ref[unit + 1].reshape(D, HALF)], axis=1)


def stages(r, comm):
    vec = r.vec

    def vrow(i):
        return vec[i : i + 1, :]

    order = []

    def stage(function):
        order.append(function)
        return function


    def norm_one(i):
        rows = rows_of(i, 128)
        unit, _ = norm_parts(r.tokens[rows, :].astype(F32))
        r.h1[rows, :] = (unit * vrow(GAIN1) + vrow(SHIFT1)).astype(BF)

    @stage
    def run_norm_one():
        r.gvec[...] = jnp.zeros_like(r.gvec)
        loop(LEN // 128, norm_one)

    def project(low, high):
        def step(i):
            rows = rows_of(i, 512)
            weights = jnp.concatenate([r.wall[u, :, :, :, :, low:high].reshape(D, high - low) for u in (0, 1, 2)], axis=1)
            q, k, v = jnp.split(dot(r.h1[rows, :], weights), 3, axis=1)
            q = (q + vec[QBIAS : QBIAS + 1, low:high]).astype(BF)
            r.q[rows, low:high] = (q * HEAD ** (-0.5)).astype(BF)
            r.k[rows, low:high] = k.astype(BF)
            r.v[rows, low:high] = (v + vec[VBIAS : VBIAS + 1, low:high]).astype(BF)

        loop(LEN // 512, step)

    @stage
    def run_project_a():
        project(0, 128)

    def project_b():
        project(128, HALF)

    def project_c(i):
        rows = rows_of(i, 512)
        out = dot(r.h1[rows, :], two_units(r.wall, 3))
        r.q[rows, HALF:D] = ((out[:, 0:HALF] + vec[QBIAS : QBIAS + 1, HALF:D]).astype(BF) * HEAD ** (-0.5)).astype(BF)
        r.k[rows, HALF:D] = out[:, HALF:D].astype(BF)
        r.v[rows, HALF:D] = (r.v[rows, HALF:D].astype(F32) + vec[VBIAS : VBIAS + 1, HALF:D]).astype(BF)

    first_lanes = lax.broadcasted_iota(jnp.int32, (QB, 128), 1) < HEAD
    lane_row = lax.broadcasted_iota(jnp.int32, (1, 128), 1)
    head_mask = [(lane_row < HEAD).astype(F32).astype(BF), (lane_row >= HEAD).astype(F32).astype(BF)]
    seen = lax.broadcasted_iota(jnp.int32, (QB, QB), 0) <= lax.broadcasted_iota(jnp.int32, (QB, QB), 1)
    seen = jnp.concatenate([seen, seen], axis=1)

    def both_heads(rows):
        return jnp.concatenate([rows * head_mask[0], rows * head_mask[1]], axis=0)

    def attend(pair):
        cols = rows_of(pair, 128)
        turned = jnp.transpose(r.v[:, cols])
        ones = jnp.ones((HEAD, LEN), BF)
        values = [jnp.concatenate([turned[:HEAD], ones], axis=0), jnp.concatenate([ones, turned[HEAD:]], axis=0)]
        for block in range(LEN // QB):
            first, finish = block * QB, (block + 1) * QB
            scores = dot(r.k[0:finish, cols], both_heads(r.q[first:finish, cols]), 1, 1)
            diag = jnp.where(seen, scores[first:finish], -jnp.inf)
            scores = diag if block == 0 else jnp.concatenate([scores[:first], diag], axis=0)
            peak = jnp.max(scores, axis=0, keepdims=True)
            raised = jnp.exp(scores - peak).astype(BF)
            parts = []
            for h in range(2):
                out = dot(values[h][:, 0:finish], raised[:, h * QB : (h + 1) * QB])
                total = out[HEAD : HEAD + 1] if h == 0 else out[0:1]
                parts.append(out[h * HEAD : (h + 1) * HEAD] * (1.0 / total))
                r.logs[pair, h : h + 1, first:finish] = peak[:, h * QB : (h + 1) * QB] + jnp.log(total)
            r.mixed[cols, first:finish] = jnp.concatenate(parts, axis=0).astype(BF)

    @stage
    def run_attend():
        def step(i):
            @pl.when(i == 1)
            def _():
                comm.before("project_b")
                project_b()

            @pl.when(i == PAIRS // 2)
            def _():
                comm.before("project_c")
                loop(LEN // 512, project_c)

            attend(i)
            comm.tick("attend", i)

        loop(PAIRS, step)

    def out_project(i):
        rows = rows_of(i, 256)
        resid = r.tokens[rows, :].astype(F32) + dot(r.mixed[:, rows], two_units(r.wall, 5), 0, 0) + vrow(OBIAS)
        r.resid[rows, :] = resid
        unit, _ = norm_parts(resid)
        r.tokens[rows, :] = (unit * vrow(GAIN2) + vrow(SHIFT2)).astype(BF)

    @stage
    def run_out_project():
        loop(LEN // 256, out_project)
    h2 = r.tokens

    alpha = 0.7978845608028654
    beta = alpha * 0.044715

    def expand(j):
        comm.tick("expand", j)
        cols = rows_of(j, D)
        bias = vec[pl.ds(EBIAS + j, 1), :]

        def step(i):
            rows = rows_of(i, 256)
            pre = dot(h2[rows, :], two_units(r.wall, 7 + 2 * j)) + bias
            square = pre * pre
            bent = jnp.tanh(pre * (alpha + beta * square))
            half = 0.5 * bent + 0.5
            slope = half + (pre * (0.5 - 0.5 * bent * bent)) * (alpha + (3.0 * beta) * square)
            r.act[rows, cols] = (pre * half).astype(BF)
            r.gp[rows, cols] = slope.astype(BF)

        loop(LEN // 256, step)

    @stage
    def run_expand():
        loop(4, expand)

    def grad_contract(w):
        y, x, c = w // 4, (w // 2) % 2, w % 2
        grad = dot(r.act[:, rows_of(w, HALF)], r.cot[...], 0, 0)
        r.gc[0, y, x, c] = grad[:, :HALF].astype(BF)
        r.gc[1, y, x, c] = grad[:, HALF:].astype(BF)
        comm.tick("grad_contract", w)

    @stage
    def run_grad_contract():
        loop(8, grad_contract)

    def column_sum(i, total):
        return total + jnp.sum(r.cot[rows_of(i, 128), :].astype(F32), axis=0, keepdims=True)

    @stage
    def run_contract_bias():
        r.gvec[G_CBIAS : G_CBIAS + 1, :] = lax.fori_loop(0, LEN // 128, column_sum, jnp.zeros((1, D), F32))

    def block_out(i):
        rows = rows_of(i, 256)
        weights = jnp.concatenate([r.wc[0].reshape(FF, HALF), r.wc[1].reshape(FF, HALF)], axis=1)
        r.leaving[rows, :] = (r.resid[rows, :] + dot(r.act[rows, :], weights) + vrow(CBIAS)).astype(BF)
        comm.tick("block_out", i)

    @stage
    def run_block_out():
        loop(LEN // 256, block_out)

    def grad_pre(j):
        y, x = j // 2, j % 2
        cols = rows_of(j, D)
        sums = jnp.zeros((1, D), F32)

        def step(i, sums):
            rows = rows_of(i, 512)
            weights = jnp.concatenate([r.wc[0, y, x].reshape(D, HALF), r.wc[1, y, x].reshape(D, HALF)], axis=1)
            grad = (dot(r.cot[rows, :], weights, 1, 1) * r.gp[rows, cols].astype(F32)).astype(BF)
            r.gp[rows, cols] = grad
            return sums + jnp.sum(grad.astype(F32), axis=0, keepdims=True)

        r.gvec[pl.ds(G_EBIAS + j, 1), :] = lax.fori_loop(0, LEN // 512, step, sums)
        comm.tick("grad_pre", j)

    @stage
    def run_grad_pre():
        loop(4, grad_pre)

    def grad_expand(j):
        grad = dot(h2[...], r.gp[:, rows_of(j, D)], 0, 0).astype(BF)
        for side in range(2):
            part = grad[:, side * HALF : (side + 1) * HALF].reshape(2, 2, 2, SLAB, HALF)
            r.ge[j // 2, :, :, :, rows_of(2 * (j % 2) + side, SLAB), :] = part
        comm.tick("grad_expand", j)

    @stage
    def run_grad_expand():
        loop(4, grad_expand)

    def grad_norm_two(i, sums):
        rows = rows_of(i, 256)
        weights = jnp.concatenate([r.wall[u].reshape(D, HALF) for u in range(7, 15)], axis=1)
        grad_in, gain, shift = norm_back(r.resid[rows, :], dot(r.gp[rows, :], weights, 1, 1), vrow(GAIN2))
        grad = r.cot[rows, :].astype(F32) + grad_in
        low = grad.astype(BF)
        r.resid[rows, :] = grad
        r.tokens[rows, :] = low
        comm.tick("grad_norm_two", i)
        return sums[0] + gain, sums[1] + shift, sums[2] + jnp.sum(low.astype(F32), axis=0, keepdims=True)

    @stage
    def run_grad_norm_two():
        zero = jnp.zeros((1, D), F32)
        gain, shift, obias = lax.fori_loop(0, LEN // 256, grad_norm_two, (zero, zero, zero))
        r.gvec[G_GAIN2 : G_GAIN2 + 1, :] = gain
        r.gvec[G_SHIFT2 : G_SHIFT2 + 1, :] = shift
        r.gvec[G_OBIAS : G_OBIAS + 1, :] = obias
    gattn = r.tokens

    def grad_output(i):
        grad = dot(r.mixed[rows_of(i, HALF), :], gattn[...]).astype(BF)
        for side in range(2):
            r.wall[12 + side, i] = grad[:, side * HALF : (side + 1) * HALF].reshape(2, 2, SLAB, HALF)

    @stage
    def run_grad_output():
        loop(2, grad_output)

    def grad_mixed(i):
        rows = rows_of(i, 512)
        grad = dot(gattn[rows, :], two_units(r.wall, 5), 1, 1).astype(BF)
        r.cot[rows, :] = grad

    @stage
    def run_grad_mixed():
        loop(LEN // 512, grad_mixed)

    def attend_back(pair):
        cols = rows_of(pair, 128)
        qsum = jnp.zeros((1, 128), F32)
        for block in reversed(range(LEN // QB)):
            first, finish = block * QB, (block + 1) * QB
            kp = r.k[0:finish, cols]
            gm = r.cot[first:finish, cols]
            qm, gh = both_heads(r.q[first:finish, cols]), both_heads(gm)
            inner = jnp.transpose(gm).astype(F32) * r.mixed[cols, first:finish].astype(F32)
            inner = [jnp.sum(inner[h * HEAD : (h + 1) * HEAD], axis=0, keepdims=True) for h in range(2)]
            log_total = jnp.concatenate([r.logs[pair, h : h + 1, first:finish] for h in range(2)], axis=1)
            probs = jnp.exp(dot(kp, qm, 1, 1) - log_total)
            diag = jnp.where(seen, probs[first:finish], 0.0)
            probs = diag if block == 0 else jnp.concatenate([probs[:first], diag], axis=0)
            grad_probs = dot(r.v[0:finish, cols], gh, 1, 1)
            grad_scores = (probs * (grad_probs - jnp.concatenate(inner, axis=1))).astype(BF)
            gq = dot(grad_scores, kp, 0, 0)
            gq = (jnp.where(first_lanes, gq[:QB], gq[QB:]) * HEAD ** (-0.5)).astype(BF)
            r.act[first:finish, cols] = gq
            qsum = qsum + jnp.sum(gq.astype(F32), axis=0, keepdims=True)
            gk = dot(grad_scores, qm)
            gv = dot(probs.astype(BF), gh)
            if finish == LEN:
                r.gk[...] = gk
                r.gv[...] = gv
            else:
                r.gk[0:finish, :] += gk
                r.gv[0:finish, :] += gv
        low = r.gv[...].astype(BF)
        r.act[:, rows_of(PAIRS + pair, 128)] = r.gk[...].astype(BF)
        r.act[:, rows_of(2 * PAIRS + pair, 128)] = low
        r.gvec[G_QBIAS : G_QBIAS + 1, cols] = qsum
        r.gvec[G_VBIAS : G_VBIAS + 1, cols] = jnp.sum(low.astype(F32), axis=0, keepdims=True)

    def grad_joint(unit, low, high):
        start = JOINT_COLS[unit]
        grad = dot(r.h1[...], r.act[:, start + low : start + high], 0, 0).astype(BF)
        r.wall[7 + unit, :, :, :, :, low:high] = grad.reshape(2, 2, 2, SLAB, high - low)

    @stage
    def run_attend_back():
        def step(i):
            attend_back(i)

            @pl.when(i == PAIRS // 2 - 1)
            def _():
                for unit in (0, 1, 2):
                    grad_joint(unit, 0, HALF)

            @pl.when(i == PAIRS - 2)
            def _():
                for unit in (3, 4):
                    grad_joint(unit, 0, 256)

            comm.tick("attend_back", i)

        loop(PAIRS, step)

    @stage
    def run_grad_joint():
        for unit in (3, 4):
            grad_joint(unit, 256, HALF)

    def grad_norm_one(i, sums):
        rows = rows_of(i, 256)
        weights = jnp.concatenate([r.wall[u].reshape(D, HALF) for u in (0, 3, 1, 4, 2)], axis=1)
        grad_hidden = dot(r.act[rows, 0 : 2 * D + HALF], weights, 1, 1)
        grad_in, gain, shift = norm_back(r.again[rows, :].astype(F32), grad_hidden, vrow(GAIN1))
        r.leaving[rows, :] = (r.resid[rows, :] + grad_in).astype(BF)
        comm.tick("grad_norm_one", i)
        return sums[0] + gain, sums[1] + shift

    @stage
    def run_grad_norm_one():
        zero = jnp.zeros((1, D), F32)
        gain, shift = lax.fori_loop(0, LEN // 256, grad_norm_one, (zero, zero))
        r.gvec[G_GAIN1 : G_GAIN1 + 1, :] = gain
        r.gvec[G_SHIFT1 : G_SHIFT1 + 1, :] = shift
    return order


def compute(r, comm):
    comm.start()
    for run in stages(r, comm):
        name = run.__name__.removeprefix("run_")
        comm.before(name)
        run()
        comm.after(name)
    comm.finish()


class Refs:
    def __init__(self, **refs):
        self.__dict__.update(refs)


STATE = dict(
    tokens=((LEN, D), BF),
    cot=((LEN, D), BF),
    wall=((UNITS, 2, 2, 2, SLAB, HALF), BF),
    wc=((2, 2, 2, 2, FF // 8, HALF), BF),
    vec=((VROWS, D), F32),
    gvec=((GROWS, D), F32),
    h1=((LEN, D), BF),
    q=((LEN, D), BF),
    k=((LEN, D), BF),
    v=((LEN, D), BF),
    mixed=((D, LEN), BF),
    logs=((PAIRS, 8, LEN), F32),
    resid=((LEN, D), F32),
    leaving=((LEN, D), BF),
    act=((LEN, FF), BF),
    gp=((LEN, FF), BF),
    gc=((2, 2, 2, 2, FF // 8, HALF), BF),
    gk=((LEN, 128), F32),
    gv=((LEN, 128), F32),
)
ANY = pl.BlockSpec(memory_space=pl.ANY)
VMEM = pl.BlockSpec(memory_space=pltpu.VMEM)


class Whole(Nothing):
    def __init__(self, r, sem):
        self.r, self.sem = r, sem

    def move(self, source, target):
        copy = pltpu.make_async_copy(source, target, self.sem)
        copy.start()
        copy.wait()

    def start(self):
        r = self.r
        for source, target in (
            (r.tokens_in, r.tokens), (r.first_in, r.v.at[:, HALF:D]), (r.cot_in, r.cot),
            (r.wall_in, r.wall), (r.wc_in, r.wc), (r.vec_in, r.vec),
        ):
            self.move(source, target)

    def before(self, what):
        if what == "grad_norm_one":
            self.move(self.r.tokens_in, self.r.again)

    def after(self, what):
        r = self.r
        if what == "block_out":
            self.move(r.leaving, r.block_output)
        elif what == "grad_norm_one":
            self.move(r.leaving, r.grad_tokens)
        elif what == "grad_contract":
            self.move(r.gc, r.gc_out)
        elif what == "grad_expand":
            self.move(r.ge, r.ge_out)
        elif what == "grad_output":
            self.move(r.wall.at[12:14], r.gjo_out.at[5:7])
        elif what == "grad_joint":
            self.move(r.wall.at[7:12], r.gjo_out.at[0:5])
            self.move(r.act.at[:, 2 * D + HALF : 3 * D], r.grad_first)

    def finish(self):
        self.move(self.r.gvec, self.r.gvec_out)


def whole_kernel(*refs):
    names = ["tokens_in", "first_in", "cot_in", "wall_in", "wc_in", "vec_in"]
    names += ["block_output", "grad_tokens", "grad_first", "gc_out", "ge_out", "gjo_out", "gvec_out"]
    names += list(STATE) + ["sem"]
    r = Refs(**dict(zip(names, refs)))
    r.ge = r.wc
    r.again = r.gp.at[:, 0:D]
    compute(r, Whole(r, r.sem))


def units_of(matrix):
    count = matrix.shape[1] // HALF
    return matrix.reshape(2, 2, 2, SLAB, count, HALF).transpose(4, 0, 1, 2, 3, 5)


def matrix_of(units):
    count = units.shape[0]
    return units.transpose(1, 2, 3, 4, 0, 5).reshape(D, count * HALF)


def outside(args):
    (tokens, first_values, cotangent, gain1, shift1, joint, qbias, vbias, output, obias,
     gain2, shift2, expand, ebias, contract, cbias) = args
    gather = functools.partial(lax.all_gather, axis_name=AXES, axis=0, tiled=True)
    scatter = functools.partial(lax.psum_scatter, axis_name=AXES, scatter_dimension=0, tiled=True)
    joint_units = units_of(gather(joint))
    wall = jnp.concatenate(
        [jnp.stack([joint_units[start // HALF] for start in JOINT_COLS]), units_of(gather(output)), units_of(gather(expand))]
    )
    wc = gather(contract).reshape(2, 2, 2, FF // 8, 2, HALF).transpose(4, 0, 1, 2, 3, 5)
    vec = jnp.stack([gather(v) for v in (gain1, shift1, qbias, vbias, obias, gain2, shift2, cbias)])
    vec = jnp.concatenate([vec, gather(ebias).reshape(4, D), jnp.zeros((4, D), BF)]).astype(F32)
    sds = jax.ShapeDtypeStruct
    block_output, grad_tokens, grad_first, gc, ge, gjo, gvec = pl.pallas_call(
        whole_kernel,
        out_shape=(
            sds((LEN, D), BF), sds((LEN, D), BF), sds((LEN, HALF), BF), sds(wc.shape, BF), sds(wc.shape, BF),
            sds((7,) + wall.shape[1:], BF), sds((GROWS, D), F32),
        ),
        in_specs=[ANY] * 6,
        out_specs=(ANY,) * 7,
        scratch_shapes=[pltpu.VMEM(*item) for item in STATE.values()] + [pltpu.SemaphoreType.DMA],
        compiler_params=pltpu.CompilerParams(vmem_limit_bytes=64 * 2**20),
    )(tokens, first_values, cotangent, wall, wc, vec)
    gc = gc.transpose(1, 2, 3, 4, 0, 5).reshape(FF, D).astype(F32)
    ge = ge.reshape(2, 8, 4, SLAB, HALF).transpose(1, 3, 0, 2, 4).reshape(D, FF).astype(F32)
    order = [JOINT_COLS.index(start * HALF) for start in range(5)]
    gj = jnp.concatenate([matrix_of(gjo[u : u + 1]) for u in order], axis=1).astype(F32)
    go = matrix_of(gjo[5:7]).astype(F32)
    small = [scatter(gvec[i]) for i in (0, 1, 8, 9, 10, 11, 12, 13)]
    return (
        block_output, grad_tokens, grad_first, small[GAIN1], small[SHIFT1], scatter(gj), small[QBIAS], small[VBIAS],
        scatter(go), small[OBIAS], small[GAIN2], small[SHIFT2], scatter(ge), scatter(gvec[G_EBIAS : G_EBIAS + 4].reshape(FF)),
        scatter(gc), small[CBIAS],
    )


class Linked:
    def __init__(self, r, depth):
        self.r, self.depth = r, depth
        wide, self.mz = lax.axis_index("wide"), lax.axis_index("narrow")
        self.my, self.mx, self.mc = wide // 4, (wide // 2) % 2, wide % 2
        self.peer = {
            "c": (wide + 1 - 2 * self.mc, self.mz),
            "x": (wide + 2 - 4 * self.mx, self.mz),
            "y": (wide + 4 - 8 * self.my, self.mz),
        }
        for d in range(1, depth):
            self.peer["z%d" % d] = (wide, lax.rem(self.mz + d, depth))
        self.far = [lax.rem(self.mz + d, depth) for d in range(depth)]
        self.share = SLAB // depth

    def remote(self, source, target, sems, place, where):
        send, recv = sems
        return pltpu.make_async_remote_copy(
            src_ref=source, dst_ref=target, send_sem=send.at[place], recv_sem=recv.at[place],
            device_id=self.peer[where], device_id_type=MESH,
        )

    def weights(self, g):
        if g[0] == "C":
            return self.r.wc, (int(g[1]),), slice(None)
        a, b, low, high = WEIGHT_SPAN[g]
        return self.r.wall, (pl.ds(a, b - a),), pl.ds(low, high - low)

    def source(self, g):
        r = self.r
        return {"J": (r.wj_in, r.sj), "O": (r.wo_in, r.so), "E": (r.we_in, r.se)}[g[0]] + (WEIGHT_COLS[g],)

    def gather_copies(self, g, step):
        r, y, x, c, both = self.r, self.my, self.mx, self.mc, slice(None)
        ref, lead, lanes = self.weights(g)
        index, late = GROUPS.index(g), g in LATE_Z
        phase = ("z", 1, 2, "c")[step] if not late else (1, 2, "z", "c")[step]
        if phase == "z":
            out = []
            for d in range(1, self.depth):
                if late:
                    view = ref.at[lead + (both, both, c, rows_of(self.mz, SLAB))]
                    parts = [(view, view)]
                elif g[0] == "C":
                    h = int(g[1])
                    parts = [(r.wc_in.at[:, h * HALF : (h + 1) * HALF], ref.at[lead + (y, x, c, rows_of(self.mz, SLAB))])]
                else:
                    rows, stage, spans = self.source(g)
                    parts = [(rows.at[:, a:b], stage.at[self.mz, :, a:b]) for a, b in spans]
                for part, (source, target) in enumerate(parts):
                    place = (index, d - 1, part)
                    out.append(self.remote(source, target, (r.gz_send, r.gz_recv), place, "z%d" % d))
            return out
        low, high = (pl.ds(0, FF // 16), pl.ds(FF // 16, FF // 16)) if g[0] == "C" else (
            pl.ds(0, SLAB // 2), pl.ds(SLAB // 2, SLAB // 2))
        if late:
            start = pl.multiple_of(self.mz * SLAB, SLAB)
            low, high = pl.ds(start, SLAB // 2), pl.ds(pl.multiple_of(start + SLAB // 2, SLAB // 2), SLAB // 2)
        if phase == 1:
            plan = [((y, x, c, low), "x", 0), ((y, x, c, high), "y", 1)]
        elif phase == 2:
            plan = [((y, both, c, low), "y", 2), ((both, x, c, high), "x", 3)]
        else:
            plan = [((both, both, c, both), "c", 4)]
        sems = (r.g_send, r.g_recv)
        views = [(ref.at[lead + at + (lanes,)], n, w) for at, w, n in plan]
        return [self.remote(view, view, sems, (index, n), w) for view, n, w in views]

    def assemble(self, g):
        r = self.r
        if g[0] == "C":
            h = int(g[1])
            r.wc[h, self.my, self.mx, self.mc, rows_of(self.mz, SLAB), :] = r.wc_in[:, h * HALF : (h + 1) * HALF]
            return
        source, stage, spans = self.source(g)
        first, _, low, high = WEIGHT_SPAN[g]
        for unit, start in enumerate(s for a, b in spans for s in range(a, b, high - low)):
            stop = start + high - low
            stage[self.mz, :, start:stop] = source[:, start:stop]
            rows = jnp.concatenate([stage[z, :, start:stop].astype(F32) for z in range(self.depth)], axis=0)
            r.wall[first + unit, self.my, self.mx, self.mc, :, low:high] = rows.astype(BF)

    def gather(self, g, step):
        if step > 0:
            for copy in self.gather_copies(g, step - 1):
                copy.wait_recv()
        if step == (0 if g in LATE_Z else 1):
            self.assemble(g)
        if step < 4:
            for copy in self.gather_copies(g, step):
                copy.start()
        else:
            for n in range(4):
                for copy in self.gather_copies(g, n):
                    copy.wait_send()

    def vec_copies(self, way, step):
        r = self.r
        held, got, kinds = self.vec_ways(way)
        kind = kinds[step]
        out = []
        for where in ["z%d" % d for d in range(1, self.depth)] if kind == "z" else [kind]:
            n = self.vec_place(where)
            out.append(self.remote(held, got(n), (r.v_send, r.v_recv), (way, n), where))
        return out

    def vec_place(self, where):
        return "cxy".index(where) if where in "cxy" else 2 + int(where[1])

    def vec_ways(self, way):
        r = self.r
        if way == 0:
            return r.vsum, lambda n: r.vgot.at[n], "zxyc"
        rows = slice(8, GROWS) if way == 1 else slice(0, 8)
        return r.gvec.at[rows, :], lambda n: r.ggot.at[n, rows, :], "cxyz"

    def vec_step(self, way, step):
        r = self.r
        held, got, kinds = self.vec_ways(way)
        if step > 0:
            for copy in self.vec_copies(way, step - 1):
                copy.wait()
            kind = kinds[step - 1]
            total = held[...].astype(F32)
            for where in ["z%d" % d for d in range(1, self.depth)] if kind == "z" else [kind]:
                total = total + got(self.vec_place(where))[...].astype(F32)
            if way == 0 and step == 4:
                r.vec[...] = total
            else:
                held[...] = total.astype(held.dtype)
        if step < 4:
            for copy in self.vec_copies(way, step):
                copy.start()

    def grads(self, g):
        r = self.r
        if g[0] in "CE":
            h = int(g[1])
            return (r.gc if g[0] == "C" else r.ge), [(h, h)], FF // 8, (0, HALF)
        a, b, low, high = GRAD_SPAN[g]
        return r.wall, [(u, u - 7) for u in range(a, b)], SLAB, (low, high)

    def scatter_copies(self, g, step):
        ref, leads, height, (left, right) = self.grads(g)
        r, index, late = self.r, SUMS.index(g), g in LATE_Z
        y, x, c, both = self.my, self.mx, self.mc, slice(None)
        lanes = pl.ds(left, right - left)
        if g[0] in "CE":
            core, one, two = r.big_core, r.big_one, r.big_two
            lead, mine = leads[0]
            if late:
                one, two = r.late_one, r.late_two
        else:
            core, one, two = r.small_core, r.small_one, r.small_two
            lead, mine = pl.ds(leads[0][0], len(leads)), pl.ds(leads[0][1], len(leads))
        phase = ("c", 1, 2, "z")[step] if not late else ("c", "z", 1, 2)[step]
        if phase == "z":
            out = []
            for d in range(1, self.depth):
                far = self.far[d]
                if late:
                    parts = [(ref.at[lead, both, both, c, rows_of(far, SLAB)], r.late.at[d - 1])]
                elif g[0] == "C":
                    parts = [(ref.at[lead, y, x, c, rows_of(far, SLAB)], r.zc.at[lead, d - 1])]
                else:
                    stage, got, spans = self.stage(g)
                    parts = [(stage.at[far, :, a:b], got.at[d - 1, :, a:b]) for a, b in spans]
                for part, (source, target) in enumerate(parts):
                    out.append(self.remote(source, target, (r.sz_send, r.sz_recv), (index, d - 1, part), "z%d" % d))
            return out
        low, high = pl.ds(0, height // 2), pl.ds(height // 2, height // 2)
        near = pl.ds(0, height // 2)
        if late:
            start = pl.multiple_of(self.mz * SLAB, SLAB)
            low, high = pl.ds(start, SLAB // 2), pl.ds(pl.multiple_of(start + SLAB // 2, SLAB // 2), SLAB // 2)
            near = pl.ds(0, SLAB // 2)
        near_mine = 0 if late else mine
        if phase == "c":
            plan = [((both, both, 1 - c, both), core.at[mine, :, :, :, lanes], "c", 0)]
        elif phase == 1:
            plan = [
                ((both, 1 - x, c, low), one.at[0, near_mine, :, near, lanes], "x", 1),
                ((1 - y, both, c, high), one.at[1, near_mine, :, near, lanes], "y", 2),
            ]
        else:
            plan = [
                ((1 - y, x, c, low), two.at[0, near_mine, near, lanes], "y", 3),
                ((y, 1 - x, c, high), two.at[1, near_mine, near, lanes], "x", 4),
            ]
        sems = (r.s_send, r.s_recv)
        return [self.remote(ref.at[(lead,) + at + (lanes,)], target, sems, (index, n), w) for at, target, w, n in plan]

    def stage(self, g):
        r = self.r
        stage, got = {"J": (r.sj, r.zj), "O": (r.so, r.zo), "E": (r.se, r.ze)}[g[0]]
        return stage, got, GRAD_COLS[g]

    def add_up(self, g, phase):
        r, y, x, c = self.r, self.my, self.mx, self.mc
        ref, leads, height, (left, right) = self.grads(g)
        late, lanes = g in LATE_Z, slice(left, right)
        core, one, two = (r.big_core, r.big_one, r.big_two) if g[0] in "CE" else (r.small_core, r.small_one, r.small_two)
        low, high, near = pl.ds(0, height // 2), pl.ds(height // 2, height // 2), slice(0, height // 2)
        if late:
            start = pl.multiple_of(self.mz * SLAB, SLAB)
            low, high = pl.ds(start, SLAB // 2), pl.ds(pl.multiple_of(start + SLAB // 2, SLAB // 2), SLAB // 2)
            near = slice(0, SLAB // 2)
            one, two = r.late_one, r.late_two

        def add(at, *got):
            total = ref[at].astype(F32)
            for item in got:
                total = total + item.astype(F32)
            ref[at] = total.astype(BF)

        for u, v in leads:
            w = 0 if late else v
            if phase == "c":
                def step(i, u=u, v=v):
                    add((u, i // 2, i % 2, c, slice(None), lanes), core[v, i // 2, i % 2, :, lanes])

                loop(4, step)
            elif phase == "z":
                def step(i, u=u):
                    rows = rows_of(self.mz, SLAB)
                    got = [r.late[d, i // 2, i % 2] for d in range(self.depth - 1)]
                    add((u, i // 2, i % 2, c, rows, lanes), *got)

                loop(4, step)
            elif phase == 1:
                def step(i, u=u, w=w):
                    add((u, i, x, c, low, lanes), one[0, w, i, near, lanes])
                    add((u, y, i, c, high, lanes), one[1, w, i, near, lanes])

                loop(2, step)
            elif g[0] == "C":
                if not late:
                    add((u, y, x, c, low), two[0, w])
                    add((u, y, x, c, high), two[1, w])
                else:
                    for part, (rows, half) in enumerate(((slice(0, SLAB // 2), low), (slice(SLAB // 2, SLAB), high))):
                        total = ref[u, y, x, c, half, :].astype(F32) + two[part, w, near, :].astype(F32)
                        r.gc_out[rows, u * HALF : (u + 1) * HALF] = total
        if phase == 2 and g[0] != "C":
            stage, _, spans = self.stage(g)
            places = iter([(s, s + right - left) for a, b in spans for s in range(a, b, right - left)])
            for u, v in leads:
                final = jnp.concatenate(
                    [
                        ref[u, y, x, c, half, lanes].astype(F32) + two[part, v, near, lanes].astype(F32)
                        for part, half in enumerate((low, high))
                    ],
                    axis=0,
                )
                for s in range(0, height, SLAB):
                    start, stop = next(places)
                    for z in range(self.depth):
                        rows = final[s + z * self.share : s + (z + 1) * self.share]
                        stage[z, :, start:stop] = rows.astype(BF)

    def put_out(self, g):
        r = self.r
        if g[0] == "C":
            h = int(g[1])
            total = r.gc[h, self.my, self.mx, self.mc, rows_of(self.mz, SLAB), :].astype(F32)
            for d in range(self.depth - 1):
                total = total + r.zc[h, d].astype(F32)
            r.gc_out[:, h * HALF : (h + 1) * HALF] = total
            return
        stage, got, spans = self.stage(g)
        out = {"J": r.gj_out, "O": r.go_out, "E": r.ge_out}[g[0]]
        for a, b in spans:
            total = stage[self.mz, :, a:b].astype(F32)
            for d in range(self.depth - 1):
                total = total + got[d, :, a:b].astype(F32)
            out[:, a:b] = total

    def scatter(self, g, step):
        r, late = self.r, g in LATE_Z
        phases = ("c", "z", 1, 2) if late else ("c", 1, 2, "z")
        if step > 0:
            for copy in self.scatter_copies(g, step - 1):
                copy.wait_recv()
            if phases[step - 1] == "z" and not late:
                self.put_out(g)
            else:
                self.add_up(g, phases[step - 1])
        turns = {"c": [(0, "c")], 1: [(1, "x"), (2, "y")], 2: [(3, "y"), (4, "x")], "z": []}
        if "C" + g[1] in LATE_Z:
            turns[1] = turns[2] = []
        if g[0] == "C" and step > 0:
            for n, where in turns[phases[step - 1]]:
                pl.semaphore_signal(
                    r.free_sem.at[n, int(g[1])], inc=1, device_id=self.peer[where], device_id_type=MESH
                )
        if step < 4:
            if g[0] == "E":
                for n, _ in turns[phases[step]]:
                    pl.semaphore_wait(r.free_sem.at[n, int(g[1])], 1)
            for copy in self.scatter_copies(g, step):
                copy.start()
        else:
            for n in range(4):
                for copy in self.scatter_copies(g, n):
                    copy.wait_send()

    def run(self, words):
        for word in words:
            name, step = word.split(".")
            step = int(step)
            if name[0] == "v":
                self.vec_step(int(name[1]), step)
            elif name[0] == "g":
                self.gather(name[1:], step)
            elif name[0] == "s":
                self.scatter(name[1:], step)
            elif step < 10:
                self.local(step).wait()
            else:
                self.local(step - 10).start()

    def local(self, n):
        r = self.r
        source, target = (
            (r.tokens_in, r.tokens),
            (r.first_in, r.v.at[:, HALF:D]),
            (r.cot_in, r.cot),
            (r.tokens_in, r.again),
            (r.act.at[:, 2 * D + HALF : 3 * D], r.grad_first),
            (r.leaving, r.block_output),
            (r.leaving, r.grad_tokens),
        )[n]
        return pltpu.make_async_copy(source, target, r.local_sem.at[n])

    def place_vectors(self):
        r, share = self.r, self.share
        me = lax.axis_index("wide") * self.depth + self.mz
        r.vec[...] = jnp.zeros_like(r.vec)
        for n in range(8):
            r.vec[n, 0:share] = getattr(r, "vec%d" % n)[...].astype(F32)
        r.vec[8, 0 : 4 * share] = r.vec8[...].astype(F32)
        r.vsum[0:8, :] = pltpu.roll(r.vec[0:8, :], me * share, 1).astype(BF)
        start = me * 4 * share
        wide_bias = pltpu.roll(r.vec[8:VROWS, :], lax.rem(start, D), 1)[0:1]
        rows = lax.broadcasted_iota(jnp.int32, (VROWS - 8, D), 0) == start // D
        r.vsum[8:VROWS, :] = jnp.where(rows, wide_bias, 0.0).astype(BF)

    def start(self):
        r = self.r
        for n in range(3):
            self.local(n).start()
        self.place_vectors()
        barrier = pltpu.get_barrier_semaphore()
        for where in self.peer:
            pl.semaphore_signal(barrier, inc=1, device_id=self.peer[where], device_id_type=MESH)
        pl.semaphore_wait(barrier, len(self.peer))
        self.run(PLAN["start"])

    def before(self, what):
        self.run(PLAN.get("before " + what, ()))

    def after(self, what):
        self.run(PLAN.get("after " + what, ()))

    def tick(self, what, i):
        for n in range(8):
            words = PLAN.get("%s %d" % (what, n), ())
            if words:
                @pl.when(i == n)
                def _(words=words):
                    self.run(words)

    def finish(self):
        self.run(PLAN["finish"])


WEIGHT_SPAN = dict(
    J0=(0, 3, 0, 128), J1=(0, 3, 128, 384), J2=(3, 5, 0, 384), O0=(5, 7, 0, 384),
    E0=(7, 9, 0, 384), E1=(9, 11, 0, 384), E2=(11, 13, 0, 384), E3=(13, 15, 0, 384),
)
WEIGHT_COLS = dict(
    J0=[(c, c + 128) for c in JOINT_COLS[0:3]], J1=[(c + 128, c + HALF) for c in JOINT_COLS[0:3]],
    J2=[(c, c + HALF) for c in JOINT_COLS[3:5]], O0=[(0, D)],
    E0=[(0, D)], E1=[(D, 2 * D)], E2=[(2 * D, 3 * D)], E3=[(3 * D, 4 * D)],
)
GROUPS = tuple(WEIGHT_SPAN) + ("C0", "C1")
GRAD_SPAN = dict(J0=(7, 10, 0, 384), J1=(10, 12, 0, 256), J2=(10, 12, 256, 384), O0=(12, 14, 0, 384))
GRAD_COLS = dict(
    J0=[(c, c + HALF) for c in JOINT_COLS[0:3]], J1=[(c, c + 256) for c in JOINT_COLS[3:5]],
    J2=[(c + 256, c + HALF) for c in JOINT_COLS[3:5]], O0=[(0, D)], E0=[(0, 2 * D)], E1=[(2 * D, 4 * D)],
)
SUMS = ("C0", "C1", "E0", "E1") + tuple(GRAD_SPAN)
LATE_Z = ("C1",)
PLAN = {
    "start": ("v0.0", "gC1.0", "gJ0.0", "gJ2.0", "gJ1.0", "gE0.0", "v0.1", "gO0.0", "gJ0.1", "gE3.0", "v0.2", "gC1.1", "gJ2.1", "v0.3", "local.0", "v0.4",),
    "before norm_one": ("gJ0.2", "gJ1.1", "gJ2.2", "gE2.0",),
    "after norm_one": ("gE1.0", "gJ1.2", "gJ0.3",),
    "before project_a": ("gC0.0", "gO0.1", "gJ0.4",),
    "after project_a": ("gJ2.3", "gE3.1", "gE0.1", "gE2.1",),
    "before attend": ("gJ1.3", "gO0.2",),
    "attend 0": ("gE1.1", "gJ1.4",),
    "before project_b": ("gJ2.4",),
    "attend 1": ("gC1.2", "gE2.2",),
    "attend 2": ("gO0.3", "gE0.2",),
    "before project_c": ("gE1.2", "local.1",),
    "attend 4": ("gE0.3", "gO0.4", "gC0.1",),
    "attend 5": ("gE3.2", "gE2.3",),
    "before out_project": ("gE1.3",),
    "after out_project": ("gE2.4",),
    "before expand": ("gC0.2", "gE0.4",),
    "expand 1": ("gE3.3", "gE1.4",),
    "expand 3": ("gE3.4",),
    "before grad_contract": ("local.2", "gC0.3",),
    "grad_contract 2": ("gC1.3",),
    "grad_contract 7": ("gC0.4",),
    "after grad_contract": ("sC0.0",),
    "after contract_bias": ("gC1.4",),
    "block_out 0": ("sC1.0",),
    "block_out 3": ("sC0.1",),
    "after block_out": ("local.15",),
    "before grad_expand": ("sC1.1",),
    "grad_expand 3": ("sE0.0",),
    "after grad_expand": ("sE1.0",),
    "grad_norm_two 0": ("sC0.2",),
    "after grad_norm_two": ("local.13", "sE0.1", "sE1.1",),
    "before attend_back": ("sO0.0",),
    "attend_back 0": ("sC0.3",),
    "attend_back 1": ("sO0.1", "sE0.2",),
    "attend_back 2": ("sE1.2", "sJ0.0", "sO0.2",),
    "attend_back 3": ("sJ0.1", "sE0.3", "sC1.2",),
    "attend_back 4": ("sJ1.0", "sE1.3", "sJ0.2",),
    "after attend_back": ("local.14", "v1.0", "sJ1.1",),
    "after grad_joint": ("sJ2.0", "sO0.3", "sJ0.3",),
    "before grad_norm_one": ("v1.1", "local.3", "local.4", "local.5",),
    "grad_norm_one 0": ("sJ2.1",),
    "grad_norm_one 1": ("v1.2",),
    "grad_norm_one 2": ("sC1.3", "sJ1.2",),
    "grad_norm_one 3": ("v1.3",),
    "after grad_norm_one": ("local.16", "v2.0", "v2.1", "sJ2.2", "sE0.4", "sJ1.3", "v2.2",),
    "finish": ("sJ0.4", "sE1.4", "local.6", "sJ2.3", "v1.4", "v2.3", "sC0.4", "sC1.4", "sJ2.4", "sO0.4", "sJ1.4", "v2.4",),
}


def linked_scratch(depth):
    share = SLAB // depth
    far = max(depth - 1, 1)
    dma = pltpu.SemaphoreType.DMA
    return dict(
        sj=pltpu.VMEM((depth, share, 2 * D + HALF), BF),
        so=pltpu.VMEM((depth, share, D), BF),
        se=pltpu.VMEM((depth, share, FF), BF),
        zj=pltpu.VMEM((far, share, 2 * D + HALF), BF),
        zo=pltpu.VMEM((far, share, D), BF),
        ze=pltpu.VMEM((far, share, FF), BF),
        zc=pltpu.VMEM((2 - len(LATE_Z), far, SLAB, HALF), BF),
        late=pltpu.VMEM((far, 2, 2, SLAB, HALF), BF),
        late_one=pltpu.VMEM((2, 1, 2, SLAB // 2, HALF), BF),
        late_two=pltpu.VMEM((2, 1, SLAB // 2, HALF), BF),
        big_core=pltpu.VMEM((2, 2, 2, FF // 8, HALF), BF),
        big_one=pltpu.VMEM((2, 2, 2, FF // 16, HALF), BF),
        big_two=pltpu.VMEM((2, 2, FF // 16, HALF), BF),
        small_core=pltpu.VMEM((7, 2, 2, SLAB, HALF), BF),
        small_one=pltpu.VMEM((2, 7, 2, SLAB // 2, HALF), BF),
        small_two=pltpu.VMEM((2, 7, SLAB // 2, HALF), BF),
        vsum=pltpu.VMEM((VROWS, D), BF),
        vgot=pltpu.VMEM((2 + depth, VROWS, D), BF),
        ggot=pltpu.VMEM((2 + depth, GROWS, D), F32),
        gz_send=dma((10, far, 3)), gz_recv=dma((10, far, 3)), g_send=dma((10, 5)), g_recv=dma((10, 5)),
        sz_send=dma((8, far, 3)), sz_recv=dma((8, far, 3)), s_send=dma((8, 5)), s_recv=dma((8, 5)),
        v_send=dma((3, 2 + depth)), v_recv=dma((3, 2 + depth)), local_sem=dma((7,)),
        free_sem=pltpu.SemaphoreType.REGULAR((5, 2)),
    )


def linked_kernel(depth, *refs):
    names = ["tokens_in", "first_in", "cot_in", "wj_in", "wo_in", "we_in", "wc_in"]
    names += ["vec%d" % n for n in range(9)]
    names += ["gvec_out", "block_output", "grad_tokens", "grad_first", "gj_out", "go_out", "ge_out", "gc_out"]
    names += list(STATE) + list(linked_scratch(depth))
    r = Refs(**dict(zip(names, refs)))
    r.ge = r.wc
    r.again = r.gp.at[:, 0:D]
    compute(r, Linked(r, depth))
    r.gvec_out[...] = r.gvec[...]


def closing_kernel(depth, *refs):
    gvec, moved, targets, vectors, sem = refs[0], refs[1:8], refs[8:15], refs[15:24], refs[24]
    passing = refs[25:32]
    arrive = [pltpu.make_async_copy(a, b, sem.at[0, n]) for n, (a, b) in enumerate(zip(moved, passing))]
    leave = [pltpu.make_async_copy(a, b, sem.at[1, n]) for n, (a, b) in enumerate(zip(passing, targets))]
    for copy in arrive:
        copy.start()
    me = lax.axis_index("wide") * depth + lax.axis_index("narrow")
    share = SLAB // depth
    small = pltpu.roll(gvec[0:G_EBIAS, :], lax.rem(D - me * share, D), 1)
    start = me * 4 * share
    rows = lax.broadcasted_iota(jnp.int32, (4, D), 0) == start // D
    wide_bias = jnp.sum(jnp.where(rows, gvec[G_EBIAS : G_EBIAS + 4, :], 0.0), axis=0, keepdims=True)
    wide_bias = pltpu.roll(jnp.broadcast_to(wide_bias, (8, D)), lax.rem(D - lax.rem(start, D), D), 1)
    for n, row in enumerate((G_GAIN1, G_SHIFT1, G_QBIAS, G_VBIAS, G_OBIAS, G_GAIN2, G_SHIFT2, G_CBIAS)):
        vectors[n][...] = small[row, 0:share]
    vectors[8][...] = wide_bias[0, 0 : 4 * share]
    for first, second in zip(arrive, leave):
        first.wait()
        second.start()
    for copy in leave:
        copy.wait()


def linked(depth, args):
    (tokens, first_values, cotangent, gain1, shift1, joint, qbias, vbias, output, obias,
     gain2, shift2, expand, ebias, contract, cbias) = args
    share = SLAB // depth
    sds = jax.ShapeDtypeStruct
    results = pl.pallas_call(
        functools.partial(linked_kernel, depth),
        out_shape=(
            sds((GROWS, D), F32), sds((LEN, D), BF), sds((LEN, D), BF), sds((LEN, HALF), BF), sds(joint.shape, F32),
            sds(output.shape, F32), sds(expand.shape, F32), sds(contract.shape, F32),
        ),
        in_specs=[ANY] * 3 + [VMEM] * 13,
        out_specs=(VMEM, ANY, ANY, ANY, VMEM, VMEM, VMEM, VMEM),
        scratch_shapes=[pltpu.VMEM(*item) for item in STATE.values()] + list(linked_scratch(depth).values()),
        compiler_params=pltpu.CompilerParams(
            vmem_limit_bytes=64 * 2**20, collective_id=0, has_side_effects=True
        ),
    )(tokens, first_values, cotangent, joint, output, expand, contract,
      gain1, shift1, qbias, vbias, obias, gain2, shift2, cbias, ebias)
    vectors = (sds((share,), F32),) * 8 + (sds((4 * share,), F32),)
    closed = pl.pallas_call(
        functools.partial(closing_kernel, depth),
        out_shape=tuple(sds(item.shape, item.dtype) for item in results[1:]) + vectors,
        in_specs=[VMEM] + [ANY] * 7,
        out_specs=(ANY,) * 7 + (VMEM,) * 9,
        scratch_shapes=[pltpu.SemaphoreType.DMA((2, 7))] + [pltpu.VMEM(item.shape, item.dtype) for item in results[1:]],
    )(*results)
    block_output, grad_tokens, grad_first, gj, go, ge, gc = closed[:7]
    gain1, shift1, qbias, vbias, obias, gain2, shift2, cbias, ebias = closed[7:]
    return (
        block_output, grad_tokens, grad_first, gain1, shift1, gj, qbias, vbias, go, obias, gain2, shift2, ge, ebias, gc, cbias
    )


def solution(mesh):
    split, flat = P(AXES, None), P(AXES)
    wide, depth = mesh.shape["wide"], mesh.shape["narrow"]
    if wide == 8 and SLAB % (8 * depth) == 0:
        body = lambda *args: linked(depth, args)
    else:
        body = lambda *args: outside(args)
    return jax.shard_map(
        body,
        mesh=mesh,
        in_specs=(split, split, split, flat, flat, split, flat, flat, split, flat, flat, flat, split, flat, split, flat),
        out_specs=(split, split, split, flat, flat, split, flat, flat, split, flat, flat, flat, split, flat, split, flat),
        check_vma=False,
    )
```

time: 201 us -> 172 us (0.86)
  Pallas kernels: 187 us -> 171 us
  local copies, waits for them, and re-layouts: 12.6 us -> 0 us
    pallas_call x1 -> x2, Pallas kernels: 187 us -> 171 us  [the longest x1 166 us: linked(): pl.pallas_call(functools.partial(linked_kernel, depth), out_shape=(sds((G...]
    unnamed x19 -> x0, local copies, waits for them, and re-layouts: 8.25 us -> none
where the time goes in v2:
time: 172 us
  Pallas kernels  171 us (99%)
    pallas_call x1, Pallas kernels, linked(): pl.pallas_call(functools.partial(linked_kernel, depth), out_shape=(sds((G...  166 us
    pallas_call x1, Pallas kernels, linked(): pl.pallas_call(functools.partial(closing_kernel, depth), out_shape=tuple(...  5.17 us

profile of v2, /device:TPU:0, one launch (start us, length us, event | category | flops | bytes accessed | tf_op | source)
XLA Modules:
  0.0 171.6 jit_solution(4074558922647869257)
XLA Ops:
  0.7 165.6 %shard_map.279 = (f32[24,768]{1,0:T(8,128)}, bf16[1024,768]{1,0:T(8,128)(2,1)}, bf16[1024,768]{1,0:T(8,128)(2,1)}, bf16[1024,384]{1,0:T(8,128)(2,1)}, f32[24,192...) custom-call(bf16[1024,768]{1,0:T(8,128)(2,1)} %refs_0_.1, bf16[1024,384]{1,0:T(8,128)(2,1)} %refs_1_.1, ...), custom_call_target="tpu_custom_call" | custom-call | tf_op jit(solution)/shard_map/pallas_call | solution.py:1032
  166.2 5.2 %shard_map.280 = (bf16[1024,768]{1,0:T(8,128)(2,1)}, bf16[1024,768]{1,0:T(8,128)(2,1)}, bf16[1024,384]{1,0:T(8,128)(2,1)}, f32[24,1920]{1,0:T(8,128)}, f32[24,76...) custom-call(f32[24,768]{1,0:T(8,128)} %get-tuple-element.40.refs_0_,, ...), custom_call_target="tpu_custom_call" | custom-call | tf_op jit(solution)/shard_map/pallas_call | solution.py:1047

commit v3 on v2

--- a/solution.py
+++ b/solution.py
@@ -14,7 +14,7 @@
 HALF = D // 2
 SLAB = D // 8
 PAIRS = D // (2 * HEAD)
-QB = 256
+QB = LEN // 4
 EPS = 1e-05
 BF = jnp.bfloat16
 F32 = jnp.float32
@@ -39,6 +39,19 @@
     lax.fori_loop(0, count, lambda i, c: (step(i), c)[1], 0)
 
 
+def loop_in_pairs(count, step):
+    loop(count // 2, lambda i: (step(2 * i), step(2 * i + 1)))
+
+
+def sum_in_pairs(count, step, start, after):
+    def pair(i, sums):
+        sums = step(2 * i + 1, step(2 * i, sums))
+        after(2 * i + 1)
+        return sums
+
+    return lax.fori_loop(0, count // 2, pair, start)
+
+
 def rows_of(index, size):
     return pl.ds(pl.multiple_of(index * size, size), size)
 
@@ -85,10 +98,17 @@
         unit, _ = norm_parts(r.tokens[rows, :].astype(F32))
         r.h1[rows, :] = (unit * vrow(GAIN1) + vrow(SHIFT1)).astype(BF)
 
+    def column_sum(i, total):
+        return total + jnp.sum(r.cot[rows_of(i, 128), :].astype(F32), axis=0, keepdims=True)
+
+    @stage
+    def run_contract_bias():
+        r.gvec[...] = jnp.zeros_like(r.gvec)
+        r.gvec[G_CBIAS : G_CBIAS + 1, :] = lax.fori_loop(0, LEN // 128, column_sum, jnp.zeros((1, D), F32))
+
     @stage
     def run_norm_one():
-        r.gvec[...] = jnp.zeros_like(r.gvec)
-        loop(LEN // 128, norm_one)
+        loop_in_pairs(LEN // 128, norm_one)
 
     def project(low, high):
         def step(i):
@@ -130,7 +150,9 @@
         turned = jnp.transpose(r.v[:, cols])
         ones = jnp.ones((HEAD, LEN), BF)
         values = [jnp.concatenate([turned[:HEAD], ones], axis=0), jnp.concatenate([ones, turned[HEAD:]], axis=0)]
-        for block in range(LEN // QB):
+        for block in (3, 2, 1, 0):
+            if block == 2:
+                comm.tick("attend_m", pair)
             first, finish = block * QB, (block + 1) * QB
             scores = dot(r.k[0:finish, cols], both_heads(r.q[first:finish, cols]), 1, 1)
             diag = jnp.where(seen, scores[first:finish], -jnp.inf)
@@ -179,7 +201,7 @@
     beta = alpha * 0.044715
 
     def expand(j):
-        comm.tick("expand", j)
+        comm.tick("expand_a", j)
         cols = rows_of(j, D)
         bias = vec[pl.ds(EBIAS + j, 1), :]
 
@@ -193,34 +215,19 @@
             r.act[rows, cols] = (pre * half).astype(BF)
             r.gp[rows, cols] = slope.astype(BF)
 
-        loop(LEN // 256, step)
+        loop_in_pairs(LEN // 256, step)
+        comm.tick("expand_b", j)
+        r.gc[j // 2, j % 2] = dot(r.act[:, cols], r.cot[...], 0, 0).astype(BF).reshape(2, FF // 8, D)
+        comm.tick("expand_c", j)
 
     @stage
     def run_expand():
         loop(4, expand)
 
-    def grad_contract(w):
-        y, x, c = w // 4, (w // 2) % 2, w % 2
-        grad = dot(r.act[:, rows_of(w, HALF)], r.cot[...], 0, 0)
-        r.gc[0, y, x, c] = grad[:, :HALF].astype(BF)
-        r.gc[1, y, x, c] = grad[:, HALF:].astype(BF)
-        comm.tick("grad_contract", w)
-
-    @stage
-    def run_grad_contract():
-        loop(8, grad_contract)
-
-    def column_sum(i, total):
-        return total + jnp.sum(r.cot[rows_of(i, 128), :].astype(F32), axis=0, keepdims=True)
-
-    @stage
-    def run_contract_bias():
-        r.gvec[G_CBIAS : G_CBIAS + 1, :] = lax.fori_loop(0, LEN // 128, column_sum, jnp.zeros((1, D), F32))
-
     def block_out(i):
         rows = rows_of(i, 256)
-        weights = jnp.concatenate([r.wc[0].reshape(FF, HALF), r.wc[1].reshape(FF, HALF)], axis=1)
-        r.leaving[rows, :] = (r.resid[rows, :] + dot(r.act[rows, :], weights) + vrow(CBIAS)).astype(BF)
+        out = r.resid[rows, :] + dot(r.act[rows, :], r.wc[...].reshape(FF, D)) + vrow(CBIAS)
+        r.act[rows, 0:D] = out.astype(BF)
         comm.tick("block_out", i)
 
     @stage
@@ -228,34 +235,26 @@
         loop(LEN // 256, block_out)
 
     def grad_pre(j):
-        y, x = j // 2, j % 2
         cols = rows_of(j, D)
-        sums = jnp.zeros((1, D), F32)
 
         def step(i, sums):
             rows = rows_of(i, 512)
-            weights = jnp.concatenate([r.wc[0, y, x].reshape(D, HALF), r.wc[1, y, x].reshape(D, HALF)], axis=1)
-            grad = (dot(r.cot[rows, :], weights, 1, 1) * r.gp[rows, cols].astype(F32)).astype(BF)
+            grad = dot(r.cot[rows, :], r.wc[j // 2, j % 2].reshape(D, D), 1, 1) * r.gp[rows, cols].astype(F32)
+            grad = grad.astype(BF)
             r.gp[rows, cols] = grad
             return sums + jnp.sum(grad.astype(F32), axis=0, keepdims=True)
 
-        r.gvec[pl.ds(G_EBIAS + j, 1), :] = lax.fori_loop(0, LEN // 512, step, sums)
+        r.gvec[pl.ds(G_EBIAS + j, 1), :] = lax.fori_loop(0, LEN // 512, step, jnp.zeros((1, D), F32))
         comm.tick("grad_pre", j)
+        grad = dot(h2[...], r.gp[:, cols], 0, 0).astype(BF)
+        for side in range(2):
+            part = grad[:, side * HALF : (side + 1) * HALF].reshape(2, 2, 2, SLAB, HALF)
+            r.ge[:, :, :, rows_of(2 * (j % 2) + side, SLAB), pl.ds(pl.multiple_of(j // 2 * HALF, HALF), HALF)] = part
+        comm.tick("grad_expand", j)
 
     @stage
     def run_grad_pre():
         loop(4, grad_pre)
-
-    def grad_expand(j):
-        grad = dot(h2[...], r.gp[:, rows_of(j, D)], 0, 0).astype(BF)
-        for side in range(2):
-            part = grad[:, side * HALF : (side + 1) * HALF].reshape(2, 2, 2, SLAB, HALF)
-            r.ge[j // 2, :, :, :, rows_of(2 * (j % 2) + side, SLAB), :] = part
-        comm.tick("grad_expand", j)
-
-    @stage
-    def run_grad_expand():
-        loop(4, grad_expand)
 
     def grad_norm_two(i, sums):
         rows = rows_of(i, 256)
@@ -265,13 +264,12 @@
         low = grad.astype(BF)
         r.resid[rows, :] = grad
         r.tokens[rows, :] = low
-        comm.tick("grad_norm_two", i)
         return sums[0] + gain, sums[1] + shift, sums[2] + jnp.sum(low.astype(F32), axis=0, keepdims=True)
 
     @stage
     def run_grad_norm_two():
         zero = jnp.zeros((1, D), F32)
-        gain, shift, obias = lax.fori_loop(0, LEN // 256, grad_norm_two, (zero, zero, zero))
+        gain, shift, obias = sum_in_pairs(LEN // 256, grad_norm_two, (zero, zero, zero), functools.partial(comm.tick, "grad_norm_two"))
         r.gvec[G_GAIN2 : G_GAIN2 + 1, :] = gain
         r.gvec[G_SHIFT2 : G_SHIFT2 + 1, :] = shift
         r.gvec[G_OBIAS : G_OBIAS + 1, :] = obias
@@ -298,7 +296,9 @@
     def attend_back(pair):
         cols = rows_of(pair, 128)
         qsum = jnp.zeros((1, 128), F32)
-        for block in reversed(range(LEN // QB)):
+        for block in (3, 2, 1, 0):
+            if block == 2:
+                comm.tick("back_m", pair)
             first, finish = block * QB, (block + 1) * QB
             kp = r.k[0:finish, cols]
             gm = r.cot[first:finish, cols]
@@ -363,14 +363,13 @@
         weights = jnp.concatenate([r.wall[u].reshape(D, HALF) for u in (0, 3, 1, 4, 2)], axis=1)
         grad_hidden = dot(r.act[rows, 0 : 2 * D + HALF], weights, 1, 1)
         grad_in, gain, shift = norm_back(r.again[rows, :].astype(F32), grad_hidden, vrow(GAIN1))
-        r.leaving[rows, :] = (r.resid[rows, :] + grad_in).astype(BF)
-        comm.tick("grad_norm_one", i)
+        r.cot[rows, :] = (r.resid[rows, :] + grad_in).astype(BF)
         return sums[0] + gain, sums[1] + shift
 
     @stage
     def run_grad_norm_one():
         zero = jnp.zeros((1, D), F32)
-        gain, shift = lax.fori_loop(0, LEN // 256, grad_norm_one, (zero, zero))
+        gain, shift = sum_in_pairs(LEN // 256, grad_norm_one, (zero, zero), functools.partial(comm.tick, "grad_norm_one"))
         r.gvec[G_GAIN1 : G_GAIN1 + 1, :] = gain
         r.gvec[G_SHIFT1 : G_SHIFT1 + 1, :] = shift
     return order
@@ -395,7 +394,7 @@
     tokens=((LEN, D), BF),
     cot=((LEN, D), BF),
     wall=((UNITS, 2, 2, 2, SLAB, HALF), BF),
-    wc=((2, 2, 2, 2, FF // 8, HALF), BF),
+    wc=((2, 2, 2, FF // 8, D), BF),
     vec=((VROWS, D), F32),
     gvec=((GROWS, D), F32),
     h1=((LEN, D), BF),
@@ -405,10 +404,10 @@
     mixed=((D, LEN), BF),
     logs=((PAIRS, 8, LEN), F32),
     resid=((LEN, D), F32),
-    leaving=((LEN, D), BF),
     act=((LEN, FF), BF),
     gp=((LEN, FF), BF),
-    gc=((2, 2, 2, 2, FF // 8, HALF), BF),
+    gc=((2, 2, 2, FF // 8, D), BF),
+    ge=((2, 2, 2, FF // 8, D), BF),
     gk=((LEN, 128), F32),
     gv=((LEN, 128), F32),
 )
@@ -440,12 +439,11 @@
     def after(self, what):
         r = self.r
         if what == "block_out":
-            self.move(r.leaving, r.block_output)
+            self.move(r.act.at[:, 0:D], r.block_output)
         elif what == "grad_norm_one":
-            self.move(r.leaving, r.grad_tokens)
-        elif what == "grad_contract":
+            self.move(r.cot, r.grad_tokens)
+        elif what == "grad_pre":
             self.move(r.gc, r.gc_out)
-        elif what == "grad_expand":
             self.move(r.ge, r.ge_out)
         elif what == "grad_output":
             self.move(r.wall.at[12:14], r.gjo_out.at[5:7])
@@ -462,7 +460,6 @@
     names += ["block_output", "grad_tokens", "grad_first", "gc_out", "ge_out", "gjo_out", "gvec_out"]
     names += list(STATE) + ["sem"]
     r = Refs(**dict(zip(names, refs)))
-    r.ge = r.wc
     r.again = r.gp.at[:, 0:D]
     compute(r, Whole(r, r.sem))
 
@@ -486,7 +483,7 @@
     wall = jnp.concatenate(
         [jnp.stack([joint_units[start // HALF] for start in JOINT_COLS]), units_of(gather(output)), units_of(gather(expand))]
     )
-    wc = gather(contract).reshape(2, 2, 2, FF // 8, 2, HALF).transpose(4, 0, 1, 2, 3, 5)
+    wc = gather(contract).reshape(2, 2, 2, FF // 8, D)
     vec = jnp.stack([gather(v) for v in (gain1, shift1, qbias, vbias, obias, gain2, shift2, cbias)])
     vec = jnp.concatenate([vec, gather(ebias).reshape(4, D), jnp.zeros((4, D), BF)]).astype(F32)
     sds = jax.ShapeDtypeStruct
@@ -501,8 +498,8 @@
         scratch_shapes=[pltpu.VMEM(*item) for item in STATE.values()] + [pltpu.SemaphoreType.DMA],
         compiler_params=pltpu.CompilerParams(vmem_limit_bytes=64 * 2**20),
     )(tokens, first_values, cotangent, wall, wc, vec)
-    gc = gc.transpose(1, 2, 3, 4, 0, 5).reshape(FF, D).astype(F32)
-    ge = ge.reshape(2, 8, 4, SLAB, HALF).transpose(1, 3, 0, 2, 4).reshape(D, FF).astype(F32)
+    gc = gc.reshape(FF, D).astype(F32)
+    ge = ge.reshape(8, 4, SLAB, 2, HALF).transpose(0, 2, 3, 1, 4).reshape(D, FF).astype(F32)
     order = [JOINT_COLS.index(start * HALF) for start in range(5)]
     gj = jnp.concatenate([matrix_of(gjo[u : u + 1]) for u in order], axis=1).astype(F32)
     go = matrix_of(gjo[5:7]).astype(F32)
@@ -523,6 +520,7 @@
             "c": (wide + 1 - 2 * self.mc, self.mz),
             "x": (wide + 2 - 4 * self.mx, self.mz),
             "y": (wide + 4 - 8 * self.my, self.mz),
+            "d": (wide + 4 - 8 * self.my + 2 - 4 * self.mx, self.mz),
         }
         for d in range(1, depth):
             self.peer["z%d" % d] = (wide, lax.rem(self.mz + d, depth))
@@ -538,7 +536,7 @@
 
     def weights(self, g):
         if g[0] == "C":
-            return self.r.wc, (int(g[1]),), slice(None)
+            return self.r.wc, (), pl.ds(C_LANES[g][0], C_LANES[g][1] - C_LANES[g][0])
         a, b, low, high = WEIGHT_SPAN[g]
         return self.r.wall, (pl.ds(a, b - a),), pl.ds(low, high - low)
 
@@ -555,11 +553,10 @@
             out = []
             for d in range(1, self.depth):
                 if late:
-                    view = ref.at[lead + (both, both, c, rows_of(self.mz, SLAB))]
+                    view = ref.at[lead + (both, both, c, rows_of(self.mz, SLAB), lanes)]
                     parts = [(view, view)]
                 elif g[0] == "C":
-                    h = int(g[1])
-                    parts = [(r.wc_in.at[:, h * HALF : (h + 1) * HALF], ref.at[lead + (y, x, c, rows_of(self.mz, SLAB))])]
+                    parts = [(r.wc_in.at[:, lanes], ref.at[lead + (y, x, c, rows_of(self.mz, SLAB), lanes)])]
                 else:
                     rows, stage, spans = self.source(g)
                     parts = [(rows.at[:, a:b], stage.at[self.mz, :, a:b]) for a, b in spans]
@@ -585,8 +582,8 @@
     def assemble(self, g):
         r = self.r
         if g[0] == "C":
-            h = int(g[1])
-            r.wc[h, self.my, self.mx, self.mc, rows_of(self.mz, SLAB), :] = r.wc_in[:, h * HALF : (h + 1) * HALF]
+            low, high = C_LANES[g]
+            r.wc[self.my, self.mx, self.mc, rows_of(self.mz, SLAB), low:high] = r.wc_in[:, low:high]
             return
         source, stage, spans = self.source(g)
         first, _, low, high = WEIGHT_SPAN[g]
@@ -610,101 +607,114 @@
                 for copy in self.gather_copies(g, n):
                     copy.wait_send()
 
+    def vec_wheres(self, kind):
+        return {"c": ["c"], "p": ["x", "y", "d"], "z": ["z%d" % d for d in range(1, self.depth)]}[kind]
+
     def vec_copies(self, way, step):
         r = self.r
         held, got, kinds = self.vec_ways(way)
-        kind = kinds[step]
         out = []
-        for where in ["z%d" % d for d in range(1, self.depth)] if kind == "z" else [kind]:
+        for where in self.vec_wheres(kinds[step]):
             n = self.vec_place(where)
             out.append(self.remote(held, got(n), (r.v_send, r.v_recv), (way, n), where))
         return out
 
     def vec_place(self, where):
-        return "cxy".index(where) if where in "cxy" else 2 + int(where[1])
+        return "cxyd".index(where) if where in "cxyd" else 3 + int(where[1])
 
     def vec_ways(self, way):
         r = self.r
-        if way == 0:
-            return r.vsum, lambda n: r.vgot.at[n], "zxyc"
-        rows = slice(8, GROWS) if way == 1 else slice(0, 8)
-        return r.gvec.at[rows, :], lambda n: r.ggot.at[n, rows, :], "cxyz"
+        if way in (0, 3):
+            return r.vsum.at[way // 3], lambda n: r.vgot.at[way // 3, n], "zpc"
+        if way == 1:
+            return r.gvec.at[8:GROWS, :], lambda n: r.ggot.at[n], "cpz"
+        return r.last, lambda n: r.lgot.at[n], "cpz"
 
     def vec_step(self, way, step):
         r = self.r
         held, got, kinds = self.vec_ways(way)
+        if way == 2 and step == 0:
+            for row in range(2):
+                for side in range(2):
+                    r.last[2 * row + side : 2 * row + side + 1, :] = r.gvec[row : row + 1, side * HALF : (side + 1) * HALF]
         if step > 0:
             for copy in self.vec_copies(way, step - 1):
                 copy.wait()
             kind = kinds[step - 1]
             total = held[...].astype(F32)
-            for where in ["z%d" % d for d in range(1, self.depth)] if kind == "z" else [kind]:
+            for where in self.vec_wheres(kind):
                 total = total + got(self.vec_place(where))[...].astype(F32)
-            if way == 0 and step == 4:
-                r.vec[...] = total
+            if step == 3 and way in (0, 3):
+                rows = slice(0, 8) if way == 0 else slice(8, 16)
+                r.vec[rows, 0:HALF] = total[0:8]
+                r.vec[rows, HALF:D] = total[8:16]
+            elif step == 3 and way == 2:
+                for row in range(2):
+                    for side in range(2):
+                        r.gvec[row : row + 1, side * HALF : (side + 1) * HALF] = total[2 * row + side : 2 * row + side + 1]
             else:
                 held[...] = total.astype(held.dtype)
-        if step < 4:
+        if step < 3:
             for copy in self.vec_copies(way, step):
                 copy.start()
 
     def grads(self, g):
         r = self.r
         if g[0] in "CE":
-            h = int(g[1])
-            return (r.gc if g[0] == "C" else r.ge), [(h, h)], FF // 8, (0, HALF)
+            low, high = C_LANES[g] if g[0] == "C" else (int(g[1]) * HALF, int(g[1]) * HALF + HALF)
+            return [(r.gc if g[0] == "C" else r.ge, (), 0, low)], FF // 8, (low, high)
         a, b, low, high = GRAD_SPAN[g]
-        return r.wall, [(u, u - 7) for u in range(a, b)], SLAB, (low, high)
+        units = [(r.wall, (u,), (u - 7) % 4 * SLAB, (u - 7) // 4 * HALF + low) for u in range(a, b)]
+        return units, SLAB, (low, high)
+
+    def slices(self, g, height, rows_at, lanes_at, wide):
+        r = self.r
+        if g in LATE_Z:
+            start, half = pl.multiple_of(self.mz * SLAB, SLAB), SLAB // 2
+            low, high = pl.ds(start, half), pl.ds(pl.multiple_of(start + half, half), half)
+            return low, high, pl.ds(0, half), pl.ds(0, wide), r.late_one, r.late_two
+        half = height // 2
+        return pl.ds(0, half), pl.ds(half, half), pl.ds(rows_at // 2, half), pl.ds(lanes_at, wide), r.near_one, r.near_two
 
     def scatter_copies(self, g, step):
-        ref, leads, height, (left, right) = self.grads(g)
+        units, height, (left, right) = self.grads(g)
         r, index, late = self.r, SUMS.index(g), g in LATE_Z
         y, x, c, both = self.my, self.mx, self.mc, slice(None)
         lanes = pl.ds(left, right - left)
-        if g[0] in "CE":
-            core, one, two = r.big_core, r.big_one, r.big_two
-            lead, mine = leads[0]
-            if late:
-                one, two = r.late_one, r.late_two
-        else:
-            core, one, two = r.small_core, r.small_one, r.small_two
-            lead, mine = pl.ds(leads[0][0], len(leads)), pl.ds(leads[0][1], len(leads))
         phase = ("c", 1, 2, "z")[step] if not late else ("c", "z", 1, 2)[step]
+        out = []
         if phase == "z":
-            out = []
             for d in range(1, self.depth):
                 far = self.far[d]
+                ref = units[0][0]
                 if late:
-                    parts = [(ref.at[lead, both, both, c, rows_of(far, SLAB)], r.late.at[d - 1])]
+                    parts = [(ref.at[both, both, c, rows_of(far, SLAB), lanes], r.late.at[d - 1])]
                 elif g[0] == "C":
-                    parts = [(ref.at[lead, y, x, c, rows_of(far, SLAB)], r.zc.at[lead, d - 1])]
+                    parts = [(ref.at[y, x, c, rows_of(far, SLAB), lanes], r.zc.at[d - 1])]
                 else:
                     stage, got, spans = self.stage(g)
                     parts = [(stage.at[far, :, a:b], got.at[d - 1, :, a:b]) for a, b in spans]
                 for part, (source, target) in enumerate(parts):
                     out.append(self.remote(source, target, (r.sz_send, r.sz_recv), (index, d - 1, part), "z%d" % d))
             return out
-        low, high = pl.ds(0, height // 2), pl.ds(height // 2, height // 2)
-        near = pl.ds(0, height // 2)
-        if late:
-            start = pl.multiple_of(self.mz * SLAB, SLAB)
-            low, high = pl.ds(start, SLAB // 2), pl.ds(pl.multiple_of(start + SLAB // 2, SLAB // 2), SLAB // 2)
-            near = pl.ds(0, SLAB // 2)
-        near_mine = 0 if late else mine
-        if phase == "c":
-            plan = [((both, both, 1 - c, both), core.at[mine, :, :, :, lanes], "c", 0)]
-        elif phase == 1:
-            plan = [
-                ((both, 1 - x, c, low), one.at[0, near_mine, :, near, lanes], "x", 1),
-                ((1 - y, both, c, high), one.at[1, near_mine, :, near, lanes], "y", 2),
-            ]
-        else:
-            plan = [
-                ((1 - y, x, c, low), two.at[0, near_mine, near, lanes], "y", 3),
-                ((y, 1 - x, c, high), two.at[1, near_mine, near, lanes], "x", 4),
-            ]
-        sems = (r.s_send, r.s_recv)
-        return [self.remote(ref.at[(lead,) + at + (lanes,)], target, sems, (index, n), w) for at, target, w, n in plan]
+        for part, (ref, lead, rows_at, lanes_at) in enumerate(units):
+            low, high, near, near_lanes, one, two = self.slices(g, height, rows_at, lanes_at, right - left)
+            if phase == "c":
+                target = r.core.at[:, :, pl.ds(rows_at, height), pl.ds(lanes_at, right - left)]
+                plan = [((both, both, 1 - c, both), target, "c", 0)]
+            elif phase == 1:
+                plan = [
+                    ((both, 1 - x, c, low), one.at[0, :, near, near_lanes], "x", 1),
+                    ((1 - y, both, c, high), one.at[1, :, near, near_lanes], "y", 2),
+                ]
+            else:
+                plan = [
+                    ((1 - y, x, c, low), two.at[0, near, near_lanes], "y", 3),
+                    ((y, 1 - x, c, high), two.at[1, near, near_lanes], "x", 4),
+                ]
+            for at, target, where, n in plan:
+                out.append(self.remote(ref.at[lead + at + (lanes,)], target, (r.s_send, r.s_recv), (index, n, part), where))
+        return out
 
     def stage(self, g):
         r = self.r
@@ -713,61 +723,55 @@
 
     def add_up(self, g, phase):
         r, y, x, c = self.r, self.my, self.mx, self.mc
-        ref, leads, height, (left, right) = self.grads(g)
-        late, lanes = g in LATE_Z, slice(left, right)
-        core, one, two = (r.big_core, r.big_one, r.big_two) if g[0] in "CE" else (r.small_core, r.small_one, r.small_two)
-        low, high, near = pl.ds(0, height // 2), pl.ds(height // 2, height // 2), slice(0, height // 2)
-        if late:
-            start = pl.multiple_of(self.mz * SLAB, SLAB)
-            low, high = pl.ds(start, SLAB // 2), pl.ds(pl.multiple_of(start + SLAB // 2, SLAB // 2), SLAB // 2)
-            near = slice(0, SLAB // 2)
-            one, two = r.late_one, r.late_two
-
-        def add(at, *got):
-            total = ref[at].astype(F32)
-            for item in got:
-                total = total + item.astype(F32)
-            ref[at] = total.astype(BF)
-
-        for u, v in leads:
-            w = 0 if late else v
-            if phase == "c":
-                def step(i, u=u, v=v):
-                    add((u, i // 2, i % 2, c, slice(None), lanes), core[v, i // 2, i % 2, :, lanes])
-
-                loop(4, step)
-            elif phase == "z":
-                def step(i, u=u):
-                    rows = rows_of(self.mz, SLAB)
-                    got = [r.late[d, i // 2, i % 2] for d in range(self.depth - 1)]
-                    add((u, i // 2, i % 2, c, rows, lanes), *got)
-
-                loop(4, step)
-            elif phase == 1:
-                def step(i, u=u, w=w):
-                    add((u, i, x, c, low, lanes), one[0, w, i, near, lanes])
-                    add((u, y, i, c, high, lanes), one[1, w, i, near, lanes])
-
-                loop(2, step)
-            elif g[0] == "C":
-                if not late:
-                    add((u, y, x, c, low), two[0, w])
-                    add((u, y, x, c, high), two[1, w])
-                else:
-                    for part, (rows, half) in enumerate(((slice(0, SLAB // 2), low), (slice(SLAB // 2, SLAB), high))):
-                        total = ref[u, y, x, c, half, :].astype(F32) + two[part, w, near, :].astype(F32)
-                        r.gc_out[rows, u * HALF : (u + 1) * HALF] = total
+        units, height, (left, right) = self.grads(g)
+        late, lanes = g in LATE_Z, pl.ds(left, right - left)
         if phase == 2 and g[0] != "C":
             stage, _, spans = self.stage(g)
             places = iter([(s, s + right - left) for a, b in spans for s in range(a, b, right - left)])
-            for u, v in leads:
-                final = jnp.concatenate(
-                    [
-                        ref[u, y, x, c, half, lanes].astype(F32) + two[part, v, near, lanes].astype(F32)
-                        for part, half in enumerate((low, high))
-                    ],
-                    axis=0,
-                )
+        for ref, lead, rows_at, lanes_at in units:
+            low, high, near, near_lanes, one, two = self.slices(g, height, rows_at, lanes_at, right - left)
+
+            def add(at, *got, ref=ref, lead=lead):
+                at = lead + at + (lanes,)
+                if len(got) == 1:
+                    ref[at] = ref[at] + got[0]
+                    return
+                total = ref[at].astype(F32)
+                for item in got:
+                    total = total + item.astype(F32)
+                ref[at] = total.astype(BF)
+
+            if phase == "c":
+                def step(i, rows_at=rows_at, lanes_at=lanes_at, add=add):
+                    got = r.core[i // 2, i % 2, pl.ds(rows_at, height), pl.ds(lanes_at, right - left)]
+                    add((i // 2, i % 2, c, slice(None)), got)
+
+                loop(4, step)
+            elif phase == "z":
+                def step(i, add=add):
+                    got = [r.late[d, i // 2, i % 2] for d in range(self.depth - 1)]
+                    add((i // 2, i % 2, c, rows_of(self.mz, SLAB)), *got)
+
+                loop(4, step)
+            elif phase == 1:
+                def step(i, add=add, low=low, high=high, near=near, near_lanes=near_lanes, one=one):
+                    add((i, x, c, low), one[0, i, near, near_lanes])
+                    add((y, i, c, high), one[1, i, near, near_lanes])
+
+                loop(2, step)
+            elif g[0] == "C" and not late:
+                add((y, x, c, low), two[0, near, near_lanes])
+                add((y, x, c, high), two[1, near, near_lanes])
+            else:
+                final = [
+                    ref[lead + (y, x, c, half, lanes)].astype(F32) + two[part, near, near_lanes].astype(F32)
+                    for part, half in enumerate((low, high))
+                ]
+                if late:
+                    r.gc_out[0 : SLAB // 2, left:right] = final[0]
+                    r.gc_out[SLAB // 2 : SLAB, left:right] = final[1]
+                    continue
+                final = jnp.concatenate(final, axis=0)
                 for s in range(0, height, SLAB):
                     start, stop = next(places)
                     for z in range(self.depth):
@@ -777,11 +781,11 @@
     def put_out(self, g):
         r = self.r
         if g[0] == "C":
-            h = int(g[1])
-            total = r.gc[h, self.my, self.mx, self.mc, rows_of(self.mz, SLAB), :].astype(F32)
+            left, right = C_LANES[g]
+            total = r.gc[self.my, self.mx, self.mc, rows_of(self.mz, SLAB), left:right].astype(F32)
             for d in range(self.depth - 1):
-                total = total + r.zc[h, d].astype(F32)
-            r.gc_out[:, h * HALF : (h + 1) * HALF] = total
+                total = total + r.zc[d].astype(F32)
+            r.gc_out[:, left:right] = total
             return
         stage, got, spans = self.stage(g)
         out = {"J": r.gj_out, "O": r.go_out, "E": r.ge_out}[g[0]]
@@ -802,23 +806,34 @@
             else:
                 self.add_up(g, phases[step - 1])
         turns = {"c": [(0, "c")], 1: [(1, "x"), (2, "y")], 2: [(3, "y"), (4, "x")], "z": []}
-        if "C" + g[1] in LATE_Z:
-            turns[1] = turns[2] = []
-        if g[0] == "C" and step > 0:
-            for n, where in turns[phases[step - 1]]:
+        own = {"c": turns["c"]} if late else turns
+        if g in OWNERS and step > 0:
+            for n, where in own.get(phases[step - 1], []):
                 pl.semaphore_signal(
-                    r.free_sem.at[n, int(g[1])], inc=1, device_id=self.peer[where], device_id_type=MESH
+                    r.free_sem.at[n, OWNERS.index(g)], inc=1, device_id=self.peer[where], device_id_type=MESH
                 )
         if step < 4:
-            if g[0] == "E":
+            for before in {"E0": ("C0",), "E1": ("C1",), "O0": ("E0", "E1")}.get(g, ()):
                 for n, _ in turns[phases[step]]:
-                    pl.semaphore_wait(r.free_sem.at[n, int(g[1])], 1)
+                    if before not in LATE_Z or n == 0:
+                        pl.semaphore_wait(r.free_sem.at[n, OWNERS.index(before)], 1)
             for copy in self.scatter_copies(g, step):
                 copy.start()
         else:
             for n in range(4):
                 for copy in self.scatter_copies(g, n):
                     copy.wait_send()
+            for copy in self.leaving(g):
+                copy.start()
+
+    def leaving(self, g):
+        r = self.r
+        source, target = {"J": (r.gj_out, r.gj_to), "O": (r.go_out, r.go_to), "E": (r.ge_out, r.ge_to), "C": (r.gc_out, r.gc_to)}[g[0]]
+        spans = [C_LANES[g]] if g[0] == "C" else GRAD_COLS[g]
+        return [
+            pltpu.make_async_copy(source.at[:, a:b], target.at[:, a:b], r.out_sem.at[SUMS.index(g), n])
+            for n, (a, b) in enumerate(spans)
+        ]
 
     def run(self, words):
         for word in words:
@@ -843,8 +858,9 @@
             (r.cot_in, r.cot),
             (r.tokens_in, r.again),
             (r.act.at[:, 2 * D + HALF : 3 * D], r.grad_first),
-            (r.leaving, r.block_output),
-            (r.leaving, r.grad_tokens),
+            (r.act.at[:, 0:D], r.block_output),
+            (r.cot, r.grad_tokens),
+            (r.wj_from, r.wj_in), (r.wo_from, r.wo_in), (r.we_from, r.we_in), (r.wc_from, r.wc_in),
         )[n]
         return pltpu.make_async_copy(source, target, r.local_sem.at[n])
 
@@ -855,20 +871,24 @@
         for n in range(8):
             r.vec[n, 0:share] = getattr(r, "vec%d" % n)[...].astype(F32)
         r.vec[8, 0 : 4 * share] = r.vec8[...].astype(F32)
-        r.vsum[0:8, :] = pltpu.roll(r.vec[0:8, :], me * share, 1).astype(BF)
+        placed = pltpu.roll(r.vec[0:8, :], me * share, 1)
+        r.vsum[0] = jnp.concatenate([placed[:, :HALF], placed[:, HALF:]], axis=0).astype(BF)
         start = me * 4 * share
         wide_bias = pltpu.roll(r.vec[8:VROWS, :], lax.rem(start, D), 1)[0:1]
         rows = lax.broadcasted_iota(jnp.int32, (VROWS - 8, D), 0) == start // D
-        r.vsum[8:VROWS, :] = jnp.where(rows, wide_bias, 0.0).astype(BF)
+        placed = jnp.where(rows, wide_bias, 0.0)
+        r.vsum[1] = jnp.concatenate([placed[:, :HALF], placed[:, HALF:]], axis=0).astype(BF)
 
     def start(self):
         r = self.r
-        for n in range(3):
-            self.local(n).start()
-        self.place_vectors()
         barrier = pltpu.get_barrier_semaphore()
         for where in self.peer:
             pl.semaphore_signal(barrier, inc=1, device_id=self.peer[where], device_id_type=MESH)
+        for n in (7, 8, 9, 10, 0, 2, 1):
+            self.local(n).start()
+        self.place_vectors()
+        for n in (7, 8, 9, 10):
+            self.local(n).wait()
         pl.semaphore_wait(barrier, len(self.peer))
         self.run(PLAN["start"])
 
@@ -888,6 +908,9 @@
 
     def finish(self):
         self.run(PLAN["finish"])
+        for g in SUMS:
+            for copy in self.leaving(g):
+                copy.wait()
 
 
 WEIGHT_SPAN = dict(
@@ -906,54 +929,63 @@
     J2=[(c + 256, c + HALF) for c in JOINT_COLS[3:5]], O0=[(0, D)], E0=[(0, 2 * D)], E1=[(2 * D, 4 * D)],
 )
 SUMS = ("C0", "C1", "E0", "E1") + tuple(GRAD_SPAN)
+C_LANES = dict(C0=(0, 512), C1=(512, 768))
+OWNERS = ("C0", "C1", "E0", "E1")
 LATE_Z = ("C1",)
 PLAN = {
-    "start": ("v0.0", "gC1.0", "gJ0.0", "gJ2.0", "gJ1.0", "gE0.0", "v0.1", "gO0.0", "gJ0.1", "gE3.0", "v0.2", "gC1.1", "gJ2.1", "v0.3", "local.0", "v0.4",),
-    "before norm_one": ("gJ0.2", "gJ1.1", "gJ2.2", "gE2.0",),
-    "after norm_one": ("gE1.0", "gJ1.2", "gJ0.3",),
-    "before project_a": ("gC0.0", "gO0.1", "gJ0.4",),
-    "after project_a": ("gJ2.3", "gE3.1", "gE0.1", "gE2.1",),
-    "before attend": ("gJ1.3", "gO0.2",),
-    "attend 0": ("gE1.1", "gJ1.4",),
-    "before project_b": ("gJ2.4",),
-    "attend 1": ("gC1.2", "gE2.2",),
-    "attend 2": ("gO0.3", "gE0.2",),
-    "before project_c": ("gE1.2", "local.1",),
-    "attend 4": ("gE0.3", "gO0.4", "gC0.1",),
-    "attend 5": ("gE3.2", "gE2.3",),
-    "before out_project": ("gE1.3",),
-    "after out_project": ("gE2.4",),
-    "before expand": ("gC0.2", "gE0.4",),
-    "expand 1": ("gE3.3", "gE1.4",),
-    "expand 3": ("gE3.4",),
-    "before grad_contract": ("local.2", "gC0.3",),
-    "grad_contract 2": ("gC1.3",),
-    "grad_contract 7": ("gC0.4",),
-    "after grad_contract": ("sC0.0",),
-    "after contract_bias": ("gC1.4",),
-    "block_out 0": ("sC1.0",),
-    "block_out 3": ("sC0.1",),
+    "start": ("gJ0.0", "v0.0", "gC1.0", "gJ1.0", "gJ0.1", "gC1.1", "v0.1", "local.0", "gO0.0", "gJ1.1", "gE1.0",),
+    "before contract_bias": ("v0.2", "gJ0.2", "gJ2.0", "v0.3", "local.2", "gO0.1",),
+    "after contract_bias": ("gE0.0", "gJ1.2",),
+    "before norm_one": ("gJ0.3", "gO0.2",),
+    "after norm_one": ("gJ2.1", "gE1.1", "gE3.0",),
+    "before project_a": ("gJ0.4",),
+    "before attend": ("gE0.1", "v3.0", "gJ1.3", "gE2.0",),
+    "attend 0": ("gC0.0", "gO0.3", "gJ2.2",),
+    "before project_b": ("gJ1.4",),
+    "attend_m 1": ("gE1.2",),
+    "attend_m 2": ("gE3.1",),
+    "attend 2": ("gE0.2",),
+    "before project_c": ("gJ2.3", "v3.1", "gJ2.4", "local.1",),
+    "attend_m 3": ("gC1.2", "gO0.4", "gE3.2",),
+    "attend 3": ("gE2.1", "gE1.3",),
+    "attend_m 4": ("gC0.1", "gE0.3",),
+    "attend_m 5": ("v3.2",),
+    "attend 5": ("gE0.4",),
+    "after attend": ("gE3.3",),
+    "after out_project": ("gE2.2",),
+    "before expand": ("v3.3", "gE3.4",),
+    "expand_b 0": ("gC0.2", "gE1.4",),
+    "expand_b 1": ("gE2.3",),
+    "expand_a 2": ("gE2.4",),
+    "expand_b 2": ("gC1.3",),
+    "expand_b 3": ("gC0.3",),
+    "expand_c 3": ("sC1.0", "gC1.4",),
+    "after expand": ("sC0.0", "gC0.4",),
+    "block_out 2": ("sC0.1",),
     "after block_out": ("local.15",),
-    "before grad_expand": ("sC1.1",),
-    "grad_expand 3": ("sE0.0",),
-    "after grad_expand": ("sE1.0",),
-    "grad_norm_two 0": ("sC0.2",),
-    "after grad_norm_two": ("local.13", "sE0.1", "sE1.1",),
-    "before attend_back": ("sO0.0",),
-    "attend_back 0": ("sC0.3",),
-    "attend_back 1": ("sO0.1", "sE0.2",),
-    "attend_back 2": ("sE1.2", "sJ0.0", "sO0.2",),
-    "attend_back 3": ("sJ0.1", "sE0.3", "sC1.2",),
-    "attend_back 4": ("sJ1.0", "sE1.3", "sJ0.2",),
-    "after attend_back": ("local.14", "v1.0", "sJ1.1",),
-    "after grad_joint": ("sJ2.0", "sO0.3", "sJ0.3",),
-    "before grad_norm_one": ("v1.1", "local.3", "local.4", "local.5",),
-    "grad_norm_one 0": ("sJ2.1",),
-    "grad_norm_one 1": ("v1.2",),
-    "grad_norm_one 2": ("sC1.3", "sJ1.2",),
-    "grad_norm_one 3": ("v1.3",),
-    "after grad_norm_one": ("local.16", "v2.0", "v2.1", "sJ2.2", "sE0.4", "sJ1.3", "v2.2",),
-    "finish": ("sJ0.4", "sE1.4", "local.6", "sJ2.3", "v1.4", "v2.3", "sC0.4", "sC1.4", "sJ2.4", "sO0.4", "sJ1.4", "v2.4",),
+    "grad_pre 2": ("sE0.0",),
+    "grad_expand 2": ("sC0.2",),
+    "grad_pre 3": ("sC1.1",),
+    "grad_expand 3": ("sE0.1",),
+    "grad_norm_two 1": ("sE1.0",),
+    "after grad_norm_two": ("local.13", "sE1.1",),
+    "after grad_output": ("sC0.3",),
+    "before attend_back": ("sO0.0", "local.5",),
+    "back_m 0": ("sE0.2",),
+    "back_m 1": ("sE1.2",),
+    "attend_back 2": ("sO0.1", "sJ0.0", "sE1.3",),
+    "back_m 3": ("sE0.3", "sJ0.1",),
+    "back_m 4": ("sO0.2",),
+    "attend_back 4": ("sJ1.0", "sJ0.2",),
+    "back_m 5": ("sJ1.1", "sO0.3",),
+    "after attend_back": ("local.14",),
+    "before grad_joint": ("v1.0",),
+    "after grad_joint": ("sJ0.3", "v1.1",),
+    "before grad_norm_one": ("local.3", "sJ2.0", "local.4",),
+    "grad_norm_one 1": ("sJ1.2", "sJ2.1", "v1.2",),
+    "grad_norm_one 3": ("sE0.4", "sJ2.2", "sJ1.3",),
+    "after grad_norm_one": ("sC1.2", "v2.0", "v2.1", "local.16", "sJ2.3", "sC1.3",),
+    "finish": ("v1.3", "sC0.4", "sJ0.4", "sE1.4", "v2.2", "sC1.4", "sO0.4", "sJ2.4", "sJ1.4", "local.6", "v2.3",),
 }
 
 
@@ -962,39 +994,41 @@
     far = max(depth - 1, 1)
     dma = pltpu.SemaphoreType.DMA
     return dict(
+        wj_in=pltpu.VMEM((share, 2 * D + HALF), BF), wo_in=pltpu.VMEM((share, D), BF),
+        we_in=pltpu.VMEM((share, FF), BF), wc_in=pltpu.VMEM((SLAB, D), BF),
+        gj_out=pltpu.VMEM((share, 2 * D + HALF), F32), go_out=pltpu.VMEM((share, D), F32),
+        ge_out=pltpu.VMEM((share, FF), F32), gc_out=pltpu.VMEM((SLAB, D), F32),
         sj=pltpu.VMEM((depth, share, 2 * D + HALF), BF),
         so=pltpu.VMEM((depth, share, D), BF),
         se=pltpu.VMEM((depth, share, FF), BF),
         zj=pltpu.VMEM((far, share, 2 * D + HALF), BF),
         zo=pltpu.VMEM((far, share, D), BF),
         ze=pltpu.VMEM((far, share, FF), BF),
-        zc=pltpu.VMEM((2 - len(LATE_Z), far, SLAB, HALF), BF),
-        late=pltpu.VMEM((far, 2, 2, SLAB, HALF), BF),
-        late_one=pltpu.VMEM((2, 1, 2, SLAB // 2, HALF), BF),
-        late_two=pltpu.VMEM((2, 1, SLAB // 2, HALF), BF),
-        big_core=pltpu.VMEM((2, 2, 2, FF // 8, HALF), BF),
-        big_one=pltpu.VMEM((2, 2, 2, FF // 16, HALF), BF),
-        big_two=pltpu.VMEM((2, 2, FF // 16, HALF), BF),
-        small_core=pltpu.VMEM((7, 2, 2, SLAB, HALF), BF),
-        small_one=pltpu.VMEM((2, 7, 2, SLAB // 2, HALF), BF),
-        small_two=pltpu.VMEM((2, 7, SLAB // 2, HALF), BF),
-        vsum=pltpu.VMEM((VROWS, D), BF),
-        vgot=pltpu.VMEM((2 + depth, VROWS, D), BF),
-        ggot=pltpu.VMEM((2 + depth, GROWS, D), F32),
+        zc=pltpu.VMEM((far, SLAB, C_LANES["C0"][1]), BF),
+        late=pltpu.VMEM((far, 2, 2, SLAB, D - C_LANES["C1"][0]), BF),
+        late_one=pltpu.VMEM((2, 2, SLAB // 2, D - C_LANES["C1"][0]), BF),
+        late_two=pltpu.VMEM((2, SLAB // 2, D - C_LANES["C1"][0]), BF),
+        core=pltpu.VMEM((2, 2, FF // 8, D), BF),
+        near_one=pltpu.VMEM((2, 2, FF // 16, D), BF),
+        near_two=pltpu.VMEM((2, FF // 16, D), BF),
+        vsum=pltpu.VMEM((2, 16, HALF), BF),
+        vgot=pltpu.VMEM((2, 3 + depth, 16, HALF), BF),
+        ggot=pltpu.VMEM((3 + depth, GROWS - 8, D), F32),
+        last=pltpu.VMEM((8, HALF), F32),
+        lgot=pltpu.VMEM((3 + depth, 8, HALF), F32),
         gz_send=dma((10, far, 3)), gz_recv=dma((10, far, 3)), g_send=dma((10, 5)), g_recv=dma((10, 5)),
-        sz_send=dma((8, far, 3)), sz_recv=dma((8, far, 3)), s_send=dma((8, 5)), s_recv=dma((8, 5)),
-        v_send=dma((3, 2 + depth)), v_recv=dma((3, 2 + depth)), local_sem=dma((7,)),
-        free_sem=pltpu.SemaphoreType.REGULAR((5, 2)),
+        sz_send=dma((8, far, 3)), sz_recv=dma((8, far, 3)), s_send=dma((8, 5, 3)), s_recv=dma((8, 5, 3)),
+        v_send=dma((4, 3 + depth)), v_recv=dma((4, 3 + depth)), local_sem=dma((11,)), out_sem=dma((8, 3)),
+        free_sem=pltpu.SemaphoreType.REGULAR((5, 4)),
     )
 
 
 def linked_kernel(depth, *refs):
-    names = ["tokens_in", "first_in", "cot_in", "wj_in", "wo_in", "we_in", "wc_in"]
+    names = ["tokens_in", "first_in", "cot_in", "wj_from", "wo_from", "we_from", "wc_from"]
     names += ["vec%d" % n for n in range(9)]
-    names += ["gvec_out", "block_output", "grad_tokens", "grad_first", "gj_out", "go_out", "ge_out", "gc_out"]
+    names += ["gvec_out", "block_output", "grad_tokens", "grad_first", "gj_to", "go_to", "ge_to", "gc_to"]
     names += list(STATE) + list(linked_scratch(depth))
     r = Refs(**dict(zip(names, refs)))
-    r.ge = r.wc
     r.again = r.gp.at[:, 0:D]
     compute(r, Linked(r, depth))
     r.gvec_out[...] = r.gvec[...]
@@ -1035,8 +1069,8 @@
             sds((GROWS, D), F32), sds((LEN, D), BF), sds((LEN, D), BF), sds((LEN, HALF), BF), sds(joint.shape, F32),
             sds(output.shape, F32), sds(expand.shape, F32), sds(contract.shape, F32),
         ),
-        in_specs=[ANY] * 3 + [VMEM] * 13,
-        out_specs=(VMEM, ANY, ANY, ANY, VMEM, VMEM, VMEM, VMEM),
+        in_specs=[ANY] * 7 + [VMEM] * 9,
+        out_specs=(VMEM,) + (ANY,) * 7,
         scratch_shapes=[pltpu.VMEM(*item) for item in STATE.values()] + list(linked_scratch(depth).values()),
         compiler_params=pltpu.CompilerParams(
             vmem_limit_bytes=64 * 2**20, collective_id=0, has_side_effects=True

time: 172 us -> 167 us (0.971)
  Pallas kernels: 171 us -> 166 us
    pallas_call x1, Pallas kernels: 166 us -> 161 us  [linked(): pl.pallas_call(functools.partial(linked_kernel, depth), out_shape=(sds((G...]
where the time goes in v3:
time: 167 us
  Pallas kernels  166 us (99%)
    pallas_call x1, Pallas kernels, linked(): pl.pallas_call(functools.partial(linked_kernel, depth), out_shape=(sds((G...  161 us
    pallas_call x1, Pallas kernels, linked(): pl.pallas_call(functools.partial(closing_kernel, depth), out_shape=tuple(...  5.17 us

profile of v3, /device:TPU:0, one launch (start us, length us, event | category | flops | bytes accessed | tf_op | source)
XLA Modules:
  0.0 166.7 jit_solution(16754912424883707932)
XLA Ops:
  0.7 160.7 %shard_map.279 = (f32[24,768]{1,0:T(8,128)}, bf16[1024,768]{1,0:T(8,128)(2,1)}, bf16[1024,768]{1,0:T(8,128)(2,1)}, bf16[1024,384]{1,0:T(8,128)(2,1)}, f32[24,192...) custom-call(bf16[1024,768]{1,0:T(8,128)(2,1)} %refs_0_.1, bf16[1024,384]{1,0:T(8,128)(2,1)} %refs_1_.1, ...), custom_call_target="tpu_custom_call" | custom-call | tf_op jit(solution)/shard_map/pallas_call | solution.py:1066
  161.4 5.2 %shard_map.280 = (bf16[1024,768]{1,0:T(8,128)(2,1)}, bf16[1024,768]{1,0:T(8,128)(2,1)}, bf16[1024,384]{1,0:T(8,128)(2,1)}, f32[24,1920]{1,0:T(8,128)}, f32[24,76...) custom-call(f32[24,768]{1,0:T(8,128)} %get-tuple-element.40.refs_0_,, ...), custom_call_target="tpu_custom_call" | custom-call | tf_op jit(solution)/shard_map/pallas_call | solution.py:1081

commit v4 on v3

--- a/solution.py
+++ b/solution.py
@@ -244,7 +244,7 @@
             r.gp[rows, cols] = grad
             return sums + jnp.sum(grad.astype(F32), axis=0, keepdims=True)
 
-        r.gvec[pl.ds(G_EBIAS + j, 1), :] = lax.fori_loop(0, LEN // 512, step, jnp.zeros((1, D), F32))
+        r.gvec[pl.ds(G_EBIAS + j, 1), :] = step(1, step(0, jnp.zeros((1, D), F32)))
         comm.tick("grad_pre", j)
         grad = dot(h2[...], r.gp[:, cols], 0, 0).astype(BF)
         for side in range(2):
@@ -282,7 +282,7 @@
 
     @stage
     def run_grad_output():
-        loop(2, grad_output)
+        loop_in_pairs(2, grad_output)
 
     def grad_mixed(i):
         rows = rows_of(i, 512)
@@ -291,7 +291,7 @@
 
     @stage
     def run_grad_mixed():
-        loop(LEN // 512, grad_mixed)
+        loop_in_pairs(LEN // 512, grad_mixed)
 
     def attend_back(pair):
         cols = rows_of(pair, 128)
@@ -962,12 +962,10 @@
     "expand_c 3": ("sC1.0", "gC1.4",),
     "after expand": ("sC0.0", "gC0.4",),
     "block_out 2": ("sC0.1",),
-    "after block_out": ("local.15",),
-    "grad_pre 2": ("sE0.0",),
+    "after block_out": ("local.15", "sC1.1",),
+    "grad_expand 1": ("sE0.0",),
     "grad_expand 2": ("sC0.2",),
-    "grad_pre 3": ("sC1.1",),
-    "grad_expand 3": ("sE0.1",),
-    "grad_norm_two 1": ("sE1.0",),
+    "grad_expand 3": ("sE0.1", "sE1.0",),
     "after grad_norm_two": ("local.13", "sE1.1",),
     "after grad_output": ("sC0.3",),
     "before attend_back": ("sO0.0", "local.5",),

time: 167 us -> 166 us (level)
  no operation moved by 1% of the time
where the time goes in v4:
time: 166 us
  Pallas kernels  165 us (99%)
    pallas_call x1, Pallas kernels, linked(): pl.pallas_call(functools.partial(linked_kernel, depth), out_shape=(sds((G...  160 us
    pallas_call x1, Pallas kernels, linked(): pl.pallas_call(functools.partial(closing_kernel, depth), out_shape=tuple(...  5.17 us

profile of v4, /device:TPU:0, one launch (start us, length us, event | category | flops | bytes accessed | tf_op | source)
XLA Modules:
  0.0 166.3 jit_solution(12079655147457192463)
XLA Ops:
  0.7 160.3 %shard_map.279 = (f32[24,768]{1,0:T(8,128)}, bf16[1024,768]{1,0:T(8,128)(2,1)}, bf16[1024,768]{1,0:T(8,128)(2,1)}, bf16[1024,384]{1,0:T(8,128)(2,1)}, f32[24,192...) custom-call(bf16[1024,768]{1,0:T(8,128)(2,1)} %refs_0_.1, bf16[1024,384]{1,0:T(8,128)(2,1)} %refs_1_.1, ...), custom_call_target="tpu_custom_call" | custom-call | tf_op jit(solution)/shard_map/pallas_call | solution.py:1064
  161.0 5.2 %shard_map.280 = (bf16[1024,768]{1,0:T(8,128)(2,1)}, bf16[1024,768]{1,0:T(8,128)(2,1)}, bf16[1024,384]{1,0:T(8,128)(2,1)}, f32[24,1920]{1,0:T(8,128)}, f32[24,76...) custom-call(f32[24,768]{1,0:T(8,128)} %get-tuple-element.40.refs_0_,, ...), custom_call_target="tpu_custom_call" | custom-call | tf_op jit(solution)/shard_map/pallas_call | solution.py:1079
